TPU v7x, 32 devices: a whole 2x2x4 slice. The times are simulated.
32 devices in a mesh: lat: 8 (over z, y), lon: 4 (over x, core).
Axes of the slice: x: 2, y: 2, z: 4, core: 2. Of those that a mesh axis runs over, the one named last changes fastest.
Arguments:
- fields: bfloat16 [1, 256, 256, 128], P(None, 'lat', 'lon'), may hold values from -6 to 6
- cotangent: bfloat16 [1, 256, 256, 128], P(None, 'lat', 'lon'), may hold values from -6 to 6
- spectral_weight: bfloat16 [256, 2, 128, 128], P('lat'), may hold values from -0.375 to 0.375
- local_weight: bfloat16 [3, 128, 128], replicated, may hold values from -0.3125 to 0.3125
- filter_basis: bfloat16 [3, 256, 3, 17], replicated, may hold values from -0.83984375 to 0.83984375
- neighbor_rows: int32 [256, 3], replicated, may hold values from 0 to 255, as said below
Outputs:
- block_output: bfloat16 [1, 256, 256, 128], P(None, 'lat', 'lon')
- input_grad: bfloat16 [1, 256, 256, 128], P(None, 'lat', 'lon')
Inputs may be any that keep to these rules, and one draw needn't show every extreme that they name: `neighbor_rows`: row i lists the rows that feed output latitude i: its first entry is max(i - 8, 0), its last min(i + 8, 255), and every entry lies within 8 of i.
All inputs are finite; a program needn't handle non-finite values.
Results may differ from a plain program's by a relative error of at most 0.015.
Values may be sent and summed in bfloat16 or wider, within the bound.
A program may use at most 128 MiB of HBM per device.

v0:
```python
import math

import jax
import jax.numpy as jnp
from jax import lax
from jax.experimental import pallas as pl
from jax.experimental.pallas import tpu as pltpu
from jax.sharding import PartitionSpec as P

MDEV = 16
HW = 8


TANH_SCALE = 0.7978845608028654
CUBIC_TERM = 0.044715


def extended(cells, sides, width):
    for axis, dim in sides:
        count = lax.axis_size(axis)
        head = lax.slice_in_dim(cells, 0, width, axis=dim)
        tail = lax.slice_in_dim(cells, cells.shape[dim] - width, cells.shape[dim], axis=dim)
        cells = jnp.concatenate(
            [
                lax.ppermute(tail, axis, [(i, (i + 1) % count) for i in range(count)]),
                cells,
                lax.ppermute(head, axis, [((i + 1) % count, i) for i in range(count)]),
            ],
            axis=dim,
        )
    return cells


def gelu_parts(values):
    tanh_input = TANH_SCALE * (values + CUBIC_TERM * values * values * values)
    hyper = jnp.tanh(tanh_input)
    result = 0.5 * values * (1.0 + hyper)
    derivative = 0.5 * (1.0 + hyper) + 0.5 * values * (1.0 - hyper * hyper) * TANH_SCALE * (
        1.0 + 3.0 * CUBIC_TERM * values * values
    )
    return (result, derivative)


def mode_tables(lon_count, mode_count):
    angles_int = (
        jnp.arange(lon_count, dtype=jnp.int32)[:, None]
        * jnp.arange(mode_count, dtype=jnp.int32)[None, :]
        % lon_count
    )
    angles = angles_int.astype(jnp.float32) * (2.0 * math.pi / lon_count)
    stacked = jnp.stack([jnp.cos(angles), -jnp.sin(angles)], axis=1)
    orders = jnp.arange(mode_count, dtype=jnp.int32)
    factor = jnp.where(orders == 0, 1.0, 2.0).astype(jnp.float32)
    to_modes = (stacked * (2.0 * math.pi / lon_count)).astype(jnp.bfloat16)
    from_modes = (stacked * factor[None, None, :]).astype(jnp.bfloat16)
    return (to_modes, from_modes)


STEP = 16


def legendre_kernel(gain_ref, back_ref, orders_ref, trig_ref, weighted_ref, plain_ref):
    order_share, degree_count, _ = plain_ref.shape
    cosine = trig_ref[0:1, :]
    quadrature = trig_ref[1:2, :]

    def block(index, state):
        carried = []
        for e in range(order_share):
            value, previous, log_scale = state[3 * e : 3 * e + 3]
            order = orders_ref[e]
            rows = []
            for step in range(STEP):
                degree = index * STEP + step
                active = degree > order
                following = gain_ref[e, degree] * (cosine * value) - back_ref[e, degree] * previous
                previous = jnp.where(active, value, previous)
                value = jnp.where(active, following, value)
                rows.append(jnp.where(degree >= order, value, 0.0))
            stacked = jnp.concatenate(rows, axis=0) * jnp.exp(log_scale)
            place = pl.ds(pl.multiple_of(index * STEP, STEP), STEP)
            plain_ref[e, place, :] = stacked.astype(jnp.bfloat16)
            weighted_ref[e, place, :] = (stacked * quadrature).astype(jnp.bfloat16)
            largest = jnp.maximum(jnp.abs(value), jnp.abs(previous))
            carried += [value / largest, previous / largest, log_scale + jnp.log(largest)]
        return tuple(carried)

    start = []
    for e in range(order_share):
        seed = trig_ref[2 + e : 3 + e, :]
        start += [jnp.ones_like(seed), jnp.zeros_like(seed), seed]
    lax.fori_loop(0, degree_count // STEP, block, tuple(start))


def legendre_tables(orders, degree_count, lat_count):
    order_share = orders.shape[0]
    colatitude = math.pi * (jnp.arange(lat_count, dtype=jnp.float32) + 0.5) / lat_count
    sine_part = jnp.sin(colatitude)
    order_real = orders.astype(jnp.float32)
    seed_log = 0.5 * (
        jnp.log((2.0 * order_real + 1.0) / (4.0 * math.pi))
        + lax.lgamma(order_real + 0.5)
        - lax.lgamma(order_real + 1.0)
        - 0.5 * math.log(math.pi)
    )
    seed_log = seed_log[:, None] + order_real[:, None] * jnp.log(sine_part)[None, :]
    degree_real = jnp.arange(degree_count, dtype=jnp.float32)[None, :]
    order_row = order_real[:, None]
    forward_gain = jnp.sqrt(
        jnp.maximum(4.0 * degree_real * degree_real - 1.0, 1.0)
        / jnp.maximum(degree_real * degree_real - order_row * order_row, 1.0)
    )
    backward_gain = jnp.sqrt(
        jnp.maximum((degree_real - 1.0) ** 2 - order_row * order_row, 0.0)
        / jnp.maximum(4.0 * (degree_real - 1.0) ** 2 - 1.0, 1.0)
    )
    trig = jnp.concatenate(
        [
            jnp.cos(colatitude)[None, :],
            (math.pi / lat_count * sine_part)[None, :],
            seed_log,
        ],
        axis=0,
    )
    table = jax.ShapeDtypeStruct((order_share, degree_count, lat_count), jnp.bfloat16)
    smem = pl.BlockSpec(memory_space=pltpu.SMEM)
    vmem = pl.BlockSpec(memory_space=pltpu.VMEM)
    return pl.pallas_call(
        legendre_kernel,
        out_shape=(table, table),
        in_specs=[smem, smem, smem, vmem],
        out_specs=(vmem, vmem),
        name="legendre_tables",
    )(forward_gain, forward_gain * backward_gain, orders, trig)


def swap(blocks, axis):
    return lax.all_to_all(blocks, axis, split_axis=0, concat_axis=0, tiled=True)


def margin(blocks):
    return extended(blocks, (("lat", 1), ("lon", 2)), HW)


def analysis(field_blocks, dft_table, degree_table):
    partial = jnp.einsum(
        "ifc,fkjbe->jbekic", field_blocks, dft_table, preferred_element_type=jnp.float32
    ).astype(jnp.bfloat16)
    fourier = jnp.sum(swap(partial, "lon").astype(jnp.float32), axis=0).astype(jnp.bfloat16)
    columns = swap(fourier, "lat")
    degrees = jnp.einsum(
        "sekic,edlsi->dlekc", columns, degree_table, preferred_element_type=jnp.float32
    ).astype(jnp.bfloat16)
    return swap(degrees, "lat")


def synthesis(spectrum, degree_table, dft_table):
    by_degree = swap(spectrum, "lat")
    zonal_modes = jnp.einsum(
        "dlekc,edlsi->sekic", by_degree, degree_table, preferred_element_type=jnp.float32
    ).astype(jnp.bfloat16)
    by_order = swap(zonal_modes, "lat")
    lon_count = dft_table.shape[2]
    every = swap(jnp.broadcast_to(by_order[None], (lon_count,) + by_order.shape), "lon")
    return jnp.einsum(
        "jbekic,fkjbe->ifc", every, dft_table, preferred_element_type=jnp.float32
    ).astype(jnp.bfloat16)


def per_device(fields, cotangent, spectral_weight, local_weight, filter_basis, neighbor_rows):
    lat_count = lax.axis_size("lat")
    lon_count = lax.axis_size("lon")
    lat_index = lax.axis_index("lat")
    lon_index = lax.axis_index("lon")
    mem_count, lat_dev, lon_dev, channels = fields.shape
    degree_dev = spectral_weight.shape[0]
    kernel_count = filter_basis.shape[0]
    band_count = filter_basis.shape[2]
    support = filter_basis.shape[3]
    half_width = HW
    total_lat = lat_dev * lat_count
    total_lon = lon_dev * lon_count
    mode_dev = MDEV
    order_share = mode_dev // lat_count
    to_modes, from_modes = mode_tables(total_lon, mode_dev * lon_count)
    table_shape = (lon_dev, 2, lon_count, lat_count, order_share)
    to_modes = lax.dynamic_slice_in_dim(to_modes, lon_index * lon_dev, lon_dev, 0)
    from_modes = lax.dynamic_slice_in_dim(from_modes, lon_index * lon_dev, lon_dev, 0)
    to_modes = to_modes.reshape(table_shape)
    from_modes = from_modes.reshape(table_shape)
    orders = (
        lon_index * mode_dev + lat_index * order_share + jnp.arange(order_share, dtype=jnp.int32)
    )
    weighted, unweighted = legendre_tables(orders, degree_dev * lat_count, total_lat)
    degree_shape = (order_share, lat_count, degree_dev, lat_count, lat_dev)
    weighted = weighted.reshape(degree_shape)
    unweighted = unweighted.reshape(degree_shape)
    real_part = spectral_weight[:, 0]
    imag_part = spectral_weight[:, 1]
    complex_mix = jnp.stack(
        [jnp.stack([real_part, imag_part], axis=2), jnp.stack([-imag_part, real_part], axis=2)],
        axis=1,
    )
    harmonics = analysis(fields[0], to_modes, weighted)
    filtered = jnp.einsum(
        "bdekc,dkcjx->bdejx", harmonics, complex_mix, preferred_element_type=jnp.float32
    ).astype(jnp.bfloat16)
    spectral = synthesis(filtered, unweighted, from_modes)[None]
    padded = margin(fields)
    row_base = lat_index * lat_dev
    my_rows = lax.dynamic_slice_in_dim(neighbor_rows, row_base, lat_dev, 0)
    my_basis = lax.dynamic_slice_in_dim(filter_basis, row_base, lat_dev, 1)
    wide_count = lon_dev + 2 * half_width
    out_pos = jnp.arange(lon_dev, dtype=jnp.int32)[:, None, None]
    in_pos = jnp.arange(wide_count, dtype=jnp.int32)[None, :, None]
    tap_pos = jnp.arange(support, dtype=jnp.int32)[None, None, :]
    forward_pick = (in_pos - out_pos == tap_pos).astype(jnp.float32)
    local_sum = jnp.zeros((kernel_count, mem_count, lat_dev, lon_dev, channels), jnp.float32)
    for band_index in range(band_count):
        source_rows = my_rows[:, band_index] - row_base + half_width
        sources = jnp.take(padded, source_rows, axis=1)
        banded = jnp.einsum(
            "kis,fts->kift", my_basis[:, :, band_index, :].astype(jnp.float32), forward_pick
        ).astype(jnp.bfloat16)
        local_sum = local_sum + jnp.einsum(
            "kift,aitc->kaifc", banded, sources, preferred_element_type=jnp.float32
        )
    local_terms = local_sum.astype(jnp.bfloat16)
    pre_act = spectral.astype(jnp.float32) + jnp.einsum(
        "kaifc,kcd->aifd", local_terms, local_weight, preferred_element_type=jnp.float32
    )
    activation, derivative = gelu_parts(pre_act)
    block_output = (fields.astype(jnp.float32) + activation).astype(jnp.bfloat16)
    grad_mix = (cotangent.astype(jnp.float32) * derivative).astype(jnp.bfloat16)
    grad_filtered = analysis(grad_mix[0], from_modes, unweighted)
    grad_harmonics = jnp.einsum(
        "bdejx,dkcjx->bdekc", grad_filtered, complex_mix, preferred_element_type=jnp.float32
    ).astype(jnp.bfloat16)
    grad_spectral = synthesis(grad_harmonics, weighted, to_modes)[None]
    grad_padded = margin(grad_mix)
    grad_local = jnp.einsum(
        "aitd,kcd->kaitc", grad_padded, local_weight, preferred_element_type=jnp.float32
    ).astype(jnp.bfloat16)
    tall_count = lat_dev + 2 * half_width
    padded_rows = row_base - half_width + jnp.arange(tall_count, dtype=jnp.int32)
    inside = (padded_rows >= 0) & (padded_rows < total_lat)
    safe_rows = jnp.clip(padded_rows, 0, total_lat - 1)
    pad_neighbors = jnp.take(neighbor_rows, safe_rows, axis=0)
    pad_basis = jnp.take(filter_basis, safe_rows, axis=1)
    back_pick = (out_pos - in_pos + 2 * half_width == tap_pos).astype(jnp.float32)
    targets = jnp.arange(lat_dev, dtype=jnp.int32)
    grad_sum = jnp.zeros((mem_count, lat_dev, lon_dev, channels), jnp.float32)
    for band_index in range(band_count):
        banded = jnp.einsum(
            "kis,qts->kiqt", pad_basis[:, :, band_index, :].astype(jnp.float32), back_pick
        ).astype(jnp.bfloat16)
        spread = jnp.einsum(
            "kiqt,kaitc->aiqc", banded, grad_local, preferred_element_type=jnp.float32
        )
        placing = (
            (pad_neighbors[:, band_index][None, :] - row_base == targets[:, None]) & inside[None, :]
        ).astype(jnp.float32)
        grad_sum = grad_sum + jnp.einsum(
            "ji,aiqc->ajqc", placing, spread, precision=lax.Precision.HIGHEST
        )
    input_grad = (
        cotangent.astype(jnp.float32) + grad_spectral.astype(jnp.float32) + grad_sum
    ).astype(jnp.bfloat16)
    return (block_output, input_grad)


def solution(mesh):
    in_specs = (
        P(None, "lat", "lon", None),
        P(None, "lat", "lon", None),
        P("lat", None, None, None),
        P(),
        P(),
        P(),
    )
    out_specs = (P(None, "lat", "lon", None), P(None, "lat", "lon", None))
    return jax.shard_map(
        per_device, mesh=mesh, in_specs=in_specs, out_specs=out_specs, check_vma=False
    )
```

profile of v0, /device:TPU:1, one launch (start us, length us, event | category | flops | bytes accessed | tf_op | source)
XLA Modules:
  0.0 229.0 jit_solution(15309934689852098398)
XLA Ops:
  0.6 1.7 fusion.205
  2.4 2.1 collective-permute-start
  4.4 3.0 %collective-permute-start.1 = (bf16[1,8,64,128]{3,2,1,0:T(8,128)(2,1)}, bf16[1,8,64,128]{3,2,1,0:T(8,128)(2,1)}, u32[]{:S(2)}, u32[]{:S(2)}) collective-permute-start(bf16[1,8,64,128]{3,2,1,0:T(8,128)(2,1)} %get-tuple-element.28), channel_id=1, source_target_pairs={{4,0},{8,4},{12,8},{16,12},{20,16},{24,20},{28,24},{0,28},{5,1},{9... | collective-permute-start | bytes 393224 | tf_op jit(solution)/shard_map/ppermute | solution.py:27
  9.1 1.5 fusion.46
  11.9 5.2 %all-to-all-start = ((bf16[4,8,2,2,32,128]{5,4,2,1,3,0:T(8,128)(2,1)}), bf16[4,8,2,2,32,128]{5,4,2,1,3,0:T(8,128)(2,1)}, u32[]{:S(2)}, u32[]{:S(2)}) async-start(bf16[4,8,2,2,32,128]{5,4,2,1,3,0:T(8,128)(2,1)} %copy.81), calls=%async_computation | async-start | bytes 2097152 | tf_op jit(solution)/shard_map/all_to_all | solution.py:138
  19.2 1.8 convolution_convert_fusion.5
  24.0 1.7 convolution_convert_fusion.6
  25.9 4.8 %all-to-all-done = bf16[4,8,2,2,32,128]{5,4,2,1,3,0:T(8,128)(2,1)} async-done(((bf16[4,8,2,2,32,128]{5,4,2,1,3,0:T(8,128)(2,1)}), bf16[4,8,2,2,32,128]{5,4,2,1,3,0:T(8,128)(2,1)}, u32[]{:S(2)}, u32[]{:S(2)}) %all-to-all-start) | async-done | bytes 1048608 | tf_op jit(solution)/shard_map/all_to_all | solution.py:138
  30.7 1.4 reduce_sum.24
  32.9 3.4 %all-to-all-start.1 = ((bf16[8,2,2,32,128]{4,3,2,1,0:T(8,128)(2,1)}), bf16[8,2,2,32,128]{4,3,2,1,0:T(8,128)(2,1)S(1)}, u32[]{:S(2)}, u32[]{:S(2)}) async-start(bf16[8,2,2,32,128]{4,3,2,1,0:T(8,128)(2,1)} %copy.82), calls=%async_computation.1 | async-start | bytes 524288 | tf_op jit(solution)/shard_map/all_to_all | solution.py:138
  37.6 3.6 %legendre_tables.1 = (bf16[2,256,256]{2,1,0:T(8,128)(2,1)}, bf16[2,256,256]{2,1,0:T(8,128)(2,1)}) custom-call(f32[2,256]{1,0:T(2,128)} %get-tuple-element.39.gain_ref, f32[2,256]{1,0:T(2,128)} %get-tuple-element.38.back_ref, s32[2]{0:T(128)} %get-tuple-element.46.orders_ref, f32[4,256]{1,0:T(4,128)} %pad_maximum_fusion.5.trig_ref), custom_call_target="tpu_custom_call" | custom-call | tf_op jit(solution)/shard_map/legendre_tables/pallas_call | solution.py:128
  41.2 2.5 %reshape.476 = bf16[2,8,32,8,32]{4,3,2,1,0:T(8,128)(2,1)} reshape(bf16[2,256,256]{2,1,0:T(8,128)(2,1)} %get-tuple-element.6) | data formatting | bytes 524288 | tf_op jit(solution)/shard_map/reshape | solution.py:196
  43.8 1.5 slice_bitcast_fusion
  45.2 1.8 fusion.85
  48.0 5.4 %all-to-all-start.2 = ((bf16[8,32,2,2,128]{4,3,1,2,0:T(2,128)(2,1)}), bf16[8,32,2,2,128]{4,3,1,2,0:T(2,128)(2,1)S(1)}, u32[]{:S(2)}, u32[]{:S(2)}) async-start(bf16[8,32,2,2,128]{4,3,1,2,0:T(2,128)(2,1)} %copy.85), calls=%async_computation.2 | async-start | bytes 524288 | tf_op jit(solution)/shard_map/all_to_all | solution.py:138
  53.4 2.3 %maximum_bitcast_fusion = (bf16[32,1,128,2,128]{4,2,1,3,0:T(8,128)(2,1)}, bf16[32,1,128,2,128]{4,2,1,3,0:T(8,128)(2,1)}) fusion(bf16[32,128,1,128]{3,1,2,0:T(8,128)(2,1)S(1)} %copy-done.13, bf16[32,128,1,128]{3,1,2,0:T(8,128)(2,1)S(1)} %copy-done.14, bf16[32,128,1,128]{3,1,2,0:T(8,128)(2,1)S(1)} %fusion.202), kind=kLoop, calls=%fused_computation.22 | loop fusion | flops 2097152 | bytes 7340032 | tf_op jit(solution)/shard_map/stack | solution.py:200
  55.7 1.8 convolution_convert_fusion.4
  57.5 3.1 %all-to-all-done.2 = bf16[8,32,2,2,128]{4,3,1,2,0:T(2,128)(2,1)S(1)} async-done(((bf16[8,32,2,2,128]{4,3,1,2,0:T(2,128)(2,1)}), bf16[8,32,2,2,128]{4,3,1,2,0:T(2,128)(2,1)S(1)}, u32[]{:S(2)}, u32[]{:S(2)}) %all-to-all-start.2) | async-done | bytes 262176 | tf_op jit(solution)/shard_map/all_to_all | solution.py:138
  60.5 3.0 %fusion.89 = bf16[8,32,2,2,128]{4,0,2,3,1:T(8,128)(2,1)S(1)} fusion(bf16[32,1,128,2,128]{4,2,1,3,0:T(8,128)(2,1)} %get-tuple-element.21, bf16[32,1,128,2,128]{4,2,1,3,0:T(8,128)(2,1)} %get-tuple-element.20, bf16[8,32,2,2,128,1]{4,3,1,2,0,5:T(2,128)(2,1)S(1)} %bitcast.381), kind=kOutput, calls=%fused_computation.83 | convolution fusion | flops 75628544 | bytes 4718592 | tf_op jit(solution)/shard_map/bdekc,dkcjx->bdejx/dot_general | solution.py:205
  64.3 5.0 %all-to-all-start.3 = ((bf16[8,32,2,2,128]{4,1,3,2,0:T(8,128)(2,1)}), bf16[8,32,2,2,128]{4,1,3,2,0:T(8,128)(2,1)}, u32[]{:S(2)}, u32[]{:S(2)}) async-start(bf16[8,32,2,2,128]{4,1,3,2,0:T(8,128)(2,1)} %copy.87), calls=%async_computation.3 | async-start | bytes 524288 | tf_op jit(solution)/shard_map/all_to_all | solution.py:138
  69.8 2.0 copy.135
  72.9 3.7 %all-to-all-done.3 = bf16[8,32,2,2,128]{4,1,3,2,0:T(8,128)(2,1)} async-done(((bf16[8,32,2,2,128]{4,1,3,2,0:T(8,128)(2,1)}), bf16[8,32,2,2,128]{4,1,3,2,0:T(8,128)(2,1)}, u32[]{:S(2)}, u32[]{:S(2)}) %all-to-all-start.3) | async-done | bytes 262176 | tf_op jit(solution)/shard_map/all_to_all | solution.py:138
  76.5 1.4 fusion.84
  78.8 4.7 %all-to-all-start.4 = ((bf16[8,2,2,32,128]{4,2,1,3,0:T(2,128)(2,1)}), bf16[8,2,2,32,128]{4,2,1,3,0:T(2,128)(2,1)S(1)}, u32[]{:S(2)}, u32[]{:S(2)}) async-start(bf16[8,2,2,32,128]{4,2,1,3,0:T(2,128)(2,1)} %copy.90), calls=%async_computation.4 | async-start | bytes 524288 | tf_op jit(solution)/shard_map/all_to_all | solution.py:138
  84.4 2.1 collective-permute-start.2
  86.5 4.1 %all-to-all-done.4 = bf16[8,2,2,32,128]{4,2,1,3,0:T(2,128)(2,1)S(1)} async-done(((bf16[8,2,2,32,128]{4,2,1,3,0:T(2,128)(2,1)}), bf16[8,2,2,32,128]{4,2,1,3,0:T(2,128)(2,1)S(1)}, u32[]{:S(2)}, u32[]{:S(2)}) %all-to-all-start.4) | async-done | bytes 262176 | tf_op jit(solution)/shard_map/all_to_all | solution.py:138
  92.0 7.1 %all-to-all-start.5 = ((bf16[4,8,2,2,32,128]{5,1,3,2,4,0:T(8,128)(2,1)}), bf16[4,8,2,2,32,128]{5,1,3,2,4,0:T(8,128)(2,1)}, u32[]{:S(2)}, u32[]{:S(2)}) async-start(bf16[4,8,2,2,32,128]{5,1,3,2,4,0:T(8,128)(2,1)} %broadcast_in_dim.40), calls=%async_computation.5 | async-start | bytes 2097152 | tf_op jit(solution)/shard_map/all_to_all | solution.py:138
  99.2 1.5 gather_fusion.3
  100.7 1.5 gather_fusion.2
  102.2 1.5 gather_fusion.4
  103.7 2.7 %fusion.23 = f32[32,128,3,64]{1,3,2,0:T(8,128)S(1)} fusion(bf16[3,32,64,80]{3,1,2,0:T(8,128)(2,1)} %convolution_convert_fusion.5, bf16[32,80,128]{2,1,0:T(8,128)(2,1)} %gather_fusion.3, pred[32]{0:T(512)(128)(4,1)S(1)} %get-tuple-element.40), kind=kOutput, calls=%fused_computation.39 | convolution fusion | flops 126156800 | bytes 4784160 | tf_op jit(solution)/shard_map/kift,aitc->kaifc/dot_general | solution.py:225
  106.4 2.5 %fusion.25 = f32[32,128,3,64]{1,3,2,0:T(8,128)} fusion(bf16[3,32,64,80]{3,1,2,0:T(8,128)(2,1)S(1)} %copy-done.6, bf16[32,80,128]{2,1,0:T(8,128)(2,1)S(1)} %copy-done.15, pred[32]{0:T(512)(128)(4,1)S(1)} %get-tuple-element.42), kind=kOutput, calls=%fused_computation.41 | convolution fusion | flops 126156800 | bytes 4784160 | tf_op jit(solution)/shard_map/kift,aitc->kaifc/dot_general | solution.py:225
  108.9 4.0 %all-to-all-done.5 = bf16[4,8,2,2,32,128]{5,1,3,2,4,0:T(8,128)(2,1)} async-done(((bf16[4,8,2,2,32,128]{5,1,3,2,4,0:T(8,128)(2,1)}), bf16[4,8,2,2,32,128]{5,1,3,2,4,0:T(8,128)(2,1)}, u32[]{:S(2)}, u32[]{:S(2)}) %all-to-all-start.5) | async-done | bytes 1048608 | tf_op jit(solution)/shard_map/all_to_all | solution.py:138
  112.8 2.5 %fusion.60 = f32[32,64,128]{2,1,0:T(8,128)} fusion(bf16[4,8,2,2,32,128]{5,1,3,2,4,0:T(8,128)(2,1)} %all-to-all-done.5, bf16[64,2,4,8,2]{0,4,3,2,1:T(2,128)(2,1)S(1)} %bitcast.378), kind=kOutput, calls=%fused_computation.60 | convolution fusion | flops 67633152 | bytes 2113536 | tf_op jit(solution)/shard_map/jbekic,fkjbe->ifc/dot_general | solution.py:165
  115.4 6.4 %fusion.92 = (bf16[1,32,64,128]{3,2,1,0:T(8,128)(2,1)}, bf16[1,32,64,128]{3,2,1,0:T(8,128)(2,1)}) fusion(bf16[1,32,64,128]{3,2,1,0:T(8,128)(2,1)} %param.9, bf16[1,32,64,128]{3,2,1,0:T(8,128)(2,1)} %param.8, f32[32,64,128]{2,1,0:T(8,128)} %fusion.60, bf16[3,128,128]{2,1,0:T(8,128)(2,1)S(1)} %copy-done, ...), kind=kOutput, calls=%fused_computation.84 | convolution fusion | flops 336396288 | bytes 11173920 | tf_op jit(solution)/shard_map/kaifc,kcd->aifd/dot_general | solution.py:229
  121.8 1.5 fusion.47
  123.3 1.3 copy.99
  124.6 4.4 %all-to-all-start.6 = ((bf16[4,8,2,2,32,128]{5,4,2,1,3,0:T(8,128)(2,1)}), bf16[4,8,2,2,32,128]{5,4,2,1,3,0:T(8,128)(2,1)S(1)}, u32[]{:S(2)}, u32[]{:S(2)}) async-start(bf16[4,8,2,2,32,128]{5,4,2,1,3,0:T(8,128)(2,1)} %copy.99), calls=%async_computation.6 | async-start | bytes 2097152 | tf_op jit(solution)/shard_map/all_to_all | solution.py:138
  130.2 2.2 convolution_convert_fusion.2
  132.4 2.3 convolution_convert_fusion.3
  134.6 7.9 %all-to-all-done.6 = bf16[4,8,2,2,32,128]{5,4,2,1,3,0:T(8,128)(2,1)S(1)} async-done(((bf16[4,8,2,2,32,128]{5,4,2,1,3,0:T(8,128)(2,1)}), bf16[4,8,2,2,32,128]{5,4,2,1,3,0:T(8,128)(2,1)S(1)}, u32[]{:S(2)}, u32[]{:S(2)}) %all-to-all-start.6) | async-done | bytes 1048608 | tf_op jit(solution)/shard_map/all_to_all | solution.py:138
  143.5 3.4 %all-to-all-start.7 = ((bf16[8,2,2,32,128]{4,3,2,1,0:T(8,128)(2,1)}), bf16[8,2,2,32,128]{4,3,2,1,0:T(8,128)(2,1)S(1)}, u32[]{:S(2)}, u32[]{:S(2)}) async-start(bf16[8,2,2,32,128]{4,3,2,1,0:T(8,128)(2,1)} %copy.100), calls=%async_computation.7 | async-start | bytes 524288 | tf_op jit(solution)/shard_map/all_to_all | solution.py:138
  147.0 2.2 convolution_convert_fusion.1
  149.2 5.0 %all-to-all-done.7 = bf16[8,2,2,32,128]{4,3,2,1,0:T(8,128)(2,1)S(1)} async-done(((bf16[8,2,2,32,128]{4,3,2,1,0:T(8,128)(2,1)}), bf16[8,2,2,32,128]{4,3,2,1,0:T(8,128)(2,1)S(1)}, u32[]{:S(2)}, u32[]{:S(2)}) %all-to-all-start.7) | async-done | bytes 262176 | tf_op jit(solution)/shard_map/all_to_all | solution.py:138
  155.5 4.8 %all-to-all-start.8 = ((bf16[8,32,2,2,128]{4,3,1,2,0:T(2,128)(2,1)}), bf16[8,32,2,2,128]{4,3,1,2,0:T(2,128)(2,1)S(1)}, u32[]{:S(2)}, u32[]{:S(2)}) async-start(bf16[8,32,2,2,128]{4,3,1,2,0:T(2,128)(2,1)} %copy.103), calls=%async_computation.8 | async-start | bytes 524288 | tf_op jit(solution)/shard_map/all_to_all | solution.py:138
  160.4 1.5 collective-permute-start.4
  161.9 2.8 %collective-permute-start.5 = (bf16[1,8,64,128]{3,2,1,0:T(8,128)(2,1)S(1)}, bf16[1,8,64,128]{3,2,1,0:T(8,128)(2,1)S(1)}, u32[]{:S(2)}, u32[]{:S(2)}) collective-permute-start(bf16[1,8,64,128]{3,2,1,0:T(8,128)(2,1)S(1)} %get-tuple-element.27), channel_id=1, source_target_pairs={{4,0},{8,4},{12,8},{16,12},{20,16},{24,20},{28,24},{0,28},{5,1},{9... | collective-permute-start | bytes 393224 | tf_op jit(solution)/shard_map/ppermute | solution.py:27
  164.7 2.7 %copy.153 = bf16[2,8,32,8,32,1]{2,3,1,5,0,4:T(8,128)(2,1)} copy(bf16[2,8,32,8,32,1]{4,3,2,1,0,5:T(8,128)(2,1)S(1)} %bitcast.373) | data formatting | bytes 524288 | tf_op jit(solution)/shard_map/reshape | solution.py:196
  167.5 3.7 %collective-permute-done.4 = bf16[1,8,64,128]{3,2,1,0:T(8,128)(2,1)S(1)} collective-permute-done((bf16[1,8,64,128]{3,2,1,0:T(8,128)(2,1)S(1)}, bf16[1,8,64,128]{3,2,1,0:T(8,128)(2,1)S(1)}, u32[]{:S(2)}, u32[]{:S(2)}) %collective-permute-start.4) | collective-permute-done | bytes 131104 | tf_op jit(solution)/shard_map/ppermute | solution.py:25
  171.2 2.5 %collective-permute-start.6 = (bf16[1,48,8,128]{3,2,1,0:T(8,128)(2,1)S(1)}, bf16[1,48,8,128]{3,2,1,0:T(8,128)(2,1)S(1)}, u32[]{:S(2)}, u32[]{:S(2)}) collective-permute-start(bf16[1,48,8,128]{3,2,1,0:T(8,128)(2,1)S(1)} %get-tuple-element.22), channel_id=1, source_target_pairs={{0,1},{1,2},{2,3},{3,0},{4,5},{5,6},{6,7},{7,4},{8,9},{9,10},{10,1... | collective-permute-start | bytes 294920 | tf_op jit(solution)/shard_map/ppermute | solution.py:25
  173.7 3.4 %fusion.86 = bf16[8,32,2,2,128]{4,0,2,3,1:T(8,128)(2,1)S(1)} fusion(bf16[8,32,2,2,128,1]{4,3,1,2,0,5:T(2,128)(2,1)S(1)} %bitcast.380, bf16[32,1,128,2,128]{4,2,1,3,0:T(8,128)(2,1)} %get-tuple-element.21, bf16[32,1,128,2,128]{4,2,1,3,0:T(8,128)(2,1)} %get-tuple-element.20), kind=kOutput, calls=%fused_computation.82 | convolution fusion | flops 69337088 | bytes 4718592 | tf_op jit(solution)/shard_map/bdejx,dkcjx->bdekc/dot_general | solution.py:236
  178.0 3.6 %all-to-all-start.9 = ((bf16[8,32,2,2,128]{4,1,3,2,0:T(8,128)(2,1)}), bf16[8,32,2,2,128]{4,1,3,2,0:T(8,128)(2,1)S(1)}, u32[]{:S(2)}, u32[]{:S(2)}) async-start(bf16[8,32,2,2,128]{4,1,3,2,0:T(8,128)(2,1)} %copy.106), calls=%async_computation.9 | async-start | bytes 524288 | tf_op jit(solution)/shard_map/all_to_all | solution.py:138
  181.6 2.2 convolution_convert_fusion
  183.9 2.4 %fusion.36 = f32[48,64,128]{2,1,0:T(8,128)} fusion(bf16[48,80,3,128]{3,1,2,0:T(8,128)(2,1)S(1)} %convolution_convert_fusion, bf16[3,48,64,80]{3,1,2,0:T(8,128)(2,1)S(1)} %copy-done.3), kind=kOutput, calls=%fused_computation.48 | convolution fusion | flops 188743680 | bytes 5996544 | tf_op jit(solution)/shard_map/kiqt,kaitc->aiqc/dot_general | solution.py:257
  186.2 2.2 all-to-all-done.9
  188.4 1.6 fusion.82
  191.0 4.4 %all-to-all-start.10 = ((bf16[8,2,2,32,128]{4,2,1,3,0:T(2,128)(2,1)}), bf16[8,2,2,32,128]{4,2,1,3,0:T(2,128)(2,1)S(1)}, u32[]{:S(2)}, u32[]{:S(2)}) async-start(bf16[8,2,2,32,128]{4,2,1,3,0:T(2,128)(2,1)} %copy.109), calls=%async_computation.10 | async-start | bytes 524288 | tf_op jit(solution)/shard_map/all_to_all | solution.py:138
  195.4 4.1 %fusion.18 = f32[64,128,32]{1,2,0:T(8,128)} fusion(f32[48,64,128]{2,1,0:T(8,128)} %fusion.36, s32[48]{0:T(128)S(1)} %get-tuple-element.9, pred[48]{0:T(512)(128)(4,1)S(1)} %compare_and_fusion.3), kind=kOutput, calls=%fused_computation.34 | convolution fusion | flops 150998016 | bytes 2621680 | tf_op jit(solution)/shard_map/ji,aiqc->ajqc/dot_general | solution.py:263
  199.5 2.4 %fusion.41 = f32[48,64,128]{2,1,0:T(8,128)} fusion(bf16[48,80,3,128]{3,1,2,0:T(8,128)(2,1)S(1)} %convolution_convert_fusion, bf16[3,48,64,80]{3,1,2,0:T(8,128)(2,1)S(1)} %copy-done.1), kind=kOutput, calls=%fused_computation.49 | convolution fusion | flops 188743680 | bytes 5996544 | tf_op jit(solution)/shard_map/kiqt,kaitc->aiqc/dot_general | solution.py:257
  204.0 7.2 %all-to-all-start.11 = ((bf16[4,8,2,2,32,128]{5,1,3,2,4,0:T(8,128)(2,1)}), bf16[4,8,2,2,32,128]{5,1,3,2,4,0:T(8,128)(2,1)}, u32[]{:S(2)}, u32[]{:S(2)}) async-start(bf16[4,8,2,2,32,128]{5,1,3,2,4,0:T(8,128)(2,1)} %broadcast_in_dim.41), calls=%async_computation.11 | async-start | bytes 2097152 | tf_op jit(solution)/shard_map/all_to_all | solution.py:138
  211.2 4.1 %fusion.20 = f32[64,128,32]{1,2,0:T(8,128)} fusion(f32[48,64,128]{2,1,0:T(8,128)} %fusion.41, s32[48]{0:T(128)S(1)} %get-tuple-element.7, pred[48]{0:T(512)(128)(4,1)S(1)} %compare_and_fusion.3), kind=kOutput, calls=%fused_computation.36 | convolution fusion | flops 150998016 | bytes 2621680 | tf_op jit(solution)/shard_map/ji,aiqc->ajqc/dot_general | solution.py:263
  216.6 1.7 fusion.16
  218.2 6.7 %all-to-all-done.11 = bf16[4,8,2,2,32,128]{5,1,3,2,4,0:T(8,128)(2,1)} async-done(((bf16[4,8,2,2,32,128]{5,1,3,2,4,0:T(8,128)(2,1)}), bf16[4,8,2,2,32,128]{5,1,3,2,4,0:T(8,128)(2,1)}, u32[]{:S(2)}, u32[]{:S(2)}) %all-to-all-start.11) | async-done | bytes 1048608 | tf_op jit(solution)/shard_map/all_to_all | solution.py:138
  224.9 4.1 %fusion.65 = bf16[1,32,64,128]{3,2,1,0:T(8,128)(2,1)} fusion(bf16[1,32,64,128]{3,2,1,0:T(8,128)(2,1)} %param.9, f32[64,128,32]{1,2,0:T(8,128)S(1)} %fusion.16, f32[64,128,32]{1,2,0:T(8,128)S(1)} %copy-done.8, f32[64,128,32]{1,2,0:T(8,128)S(1)} %copy-done.9, bf16[4,8,2,2,32,128]{5,1,3,2,4,0:T(8,128)(2,1)} %all-to-all-done.11, ...), kind=kOutput, calls=%fused_computation.65 | convolution fusion | flops 69206016 | bytes 5259264 | tf_op jit(solution)/shard_map/jbekic,fkjbe->ifc/dot_general | solution.py:165
  (125 shorter events, 25.9 us)
Async XLA Ops:
  0.6 114.7 %copy-start = (bf16[3,128,128]{2,1,0:T(8,128)(2,1)S(1)}, bf16[3,128,128]{2,1,0:T(8,128)(2,1)}, u32[]{:S(2)}) copy-start(bf16[3,128,128]{2,1,0:T(8,128)(2,1)} %param.11) | copy-start | bytes 294916
  2.4 69.5 %collective-permute-start = (bf16[1,8,64,128]{3,2,1,0:T(8,128)(2,1)}, bf16[1,8,64,128]{3,2,1,0:T(8,128)(2,1)}, u32[]{:S(2)}, u32[]{:S(2)}) collective-permute-start(bf16[1,8,64,128]{3,2,1,0:T(8,128)(2,1)} %get-tuple-element.29), channel_id=1, source_target_pairs={{0,4},{4,8},{8,12},{12,16},{16,20},{20,24},{24,28},{28,0},{1,5},{5... | collective-permute-start | bytes 393224 | tf_op jit(solution)/shard_map/ppermute | solution.py:25
  4.4 79.0 %collective-permute-start.1 = (bf16[1,8,64,128]{3,2,1,0:T(8,128)(2,1)}, bf16[1,8,64,128]{3,2,1,0:T(8,128)(2,1)}, u32[]{:S(2)}, u32[]{:S(2)}) collective-permute-start(bf16[1,8,64,128]{3,2,1,0:T(8,128)(2,1)} %get-tuple-element.28), channel_id=1, source_target_pairs={{4,0},{8,4},{12,8},{16,12},{20,16},{24,20},{28,24},{0,28},{5,1},{9... | collective-permute-start | bytes 393224 | tf_op jit(solution)/shard_map/ppermute | solution.py:27
  8.5 0.6 copy-start.18
  10.6 7.9 %copy-start.17 = (bf16[3,256,3,17]{1,2,3,0:T(4,128)(2,1)S(1)}, bf16[3,256,3,17]{1,2,3,0:T(4,128)(2,1)}, u32[]{:S(2)}) copy-start(bf16[3,256,3,17]{1,2,3,0:T(4,128)(2,1)} %param.12) | copy-start | bytes 235012
  11.9 18.9 %all-to-all-start = ((bf16[4,8,2,2,32,128]{5,4,2,1,3,0:T(8,128)(2,1)}), bf16[4,8,2,2,32,128]{5,4,2,1,3,0:T(8,128)(2,1)}, u32[]{:S(2)}, u32[]{:S(2)}) async-start(bf16[4,8,2,2,32,128]{5,4,2,1,3,0:T(8,128)(2,1)} %copy.81), calls=%async_computation | async-start | bytes 2097152 | tf_op jit(solution)/shard_map/all_to_all | solution.py:138
  19.2 6.5 %copy-start.7 = (bf16[32,2,128,128]{3,2,1,0:T(8,128)(2,1)S(1)}, bf16[32,2,128,128]{3,2,1,0:T(8,128)(2,1)}, u32[]{:S(2)}) copy-start(bf16[32,2,128,128]{3,2,1,0:T(8,128)(2,1)} %param.10) | copy-start | bytes 6291460
  21.8 4.0 %copy-start.25 = (pred[48]{0:T(512)(128)(4,1)}, pred[48]{0:T(512)(128)(4,1)S(1)}, u32[]{:S(2)}) copy-start(pred[48]{0:T(512)(128)(4,1)S(1)} %compare_and_fusion.4) | copy-start | bytes 148
  25.9 17.8 %copy-start.24 = (s32[256,3]{0,1:T(4,128)S(1)}, s32[256,3]{0,1:T(4,128)}, u32[]{:S(2)}) copy-start(s32[256,3]{0,1:T(4,128)} %param.13) | copy-start | bytes 9220
  32.9 12.3 %all-to-all-start.1 = ((bf16[8,2,2,32,128]{4,3,2,1,0:T(8,128)(2,1)}), bf16[8,2,2,32,128]{4,3,2,1,0:T(8,128)(2,1)S(1)}, u32[]{:S(2)}, u32[]{:S(2)}) async-start(bf16[8,2,2,32,128]{4,3,2,1,0:T(8,128)(2,1)} %copy.82), calls=%async_computation.1 | async-start | bytes 524288 | tf_op jit(solution)/shard_map/all_to_all | solution.py:138
  45.2 8.1 %copy-start.13 = (bf16[32,128,1,128]{3,1,2,0:T(8,128)(2,1)S(1)}, bf16[32,128,1,128]{3,1,2,0:T(8,128)(2,1)}, u32[]{:S(2)}) copy-start(bf16[32,128,1,128]{3,1,2,0:T(8,128)(2,1)} %get-tuple-element.16) | copy-start | bytes 3145732
  45.2 8.1 %copy-start.14 = (bf16[32,128,1,128]{3,1,2,0:T(8,128)(2,1)S(1)}, bf16[32,128,1,128]{3,1,2,0:T(8,128)(2,1)}, u32[]{:S(2)}) copy-start(bf16[32,128,1,128]{3,1,2,0:T(8,128)(2,1)} %get-tuple-element.17) | copy-start | bytes 3145732
  48.0 12.6 %all-to-all-start.2 = ((bf16[8,32,2,2,128]{4,3,1,2,0:T(2,128)(2,1)}), bf16[8,32,2,2,128]{4,3,1,2,0:T(2,128)(2,1)S(1)}, u32[]{:S(2)}, u32[]{:S(2)}) async-start(bf16[8,32,2,2,128]{4,3,1,2,0:T(2,128)(2,1)} %copy.85), calls=%async_computation.2 | async-start | bytes 524288 | tf_op jit(solution)/shard_map/all_to_all | solution.py:138
  53.4 2.3 %copy-start.23 = (bf16[3,32,1,17]{1,2,3,0:T(2,128)(2,1)S(1)}, bf16[3,32,1,17]{1,2,3,0:T(2,128)(2,1)}, u32[]{:S(2)}) copy-start(bf16[3,32,1,17]{1,2,3,0:T(2,128)(2,1)} %get-tuple-element.37) | copy-start | bytes 9796
  60.5 8.8 %copy-start.21 = (bf16[2,256,256]{2,1,0:T(8,128)(2,1)S(1)}, bf16[2,256,256]{2,1,0:T(8,128)(2,1)}, u32[]{:S(2)}) copy-start(bf16[2,256,256]{2,1,0:T(8,128)(2,1)} %get-tuple-element.5) | copy-start | bytes 786436
  64.3 8.4 %copy-start.4 = (bf16[1,32,64,128]{3,2,1,0:T(8,128)(2,1)S(1)}, bf16[1,32,64,128]{3,2,1,0:T(8,128)(2,1)}, u32[]{:S(2)}) copy-start(bf16[1,32,64,128]{3,2,1,0:T(8,128)(2,1)} %param.8) | copy-start | bytes 1572868
  64.3 12.2 %all-to-all-start.3 = ((bf16[8,32,2,2,128]{4,1,3,2,0:T(8,128)(2,1)}), bf16[8,32,2,2,128]{4,1,3,2,0:T(8,128)(2,1)}, u32[]{:S(2)}, u32[]{:S(2)}) async-start(bf16[8,32,2,2,128]{4,1,3,2,0:T(8,128)(2,1)} %copy.87), calls=%async_computation.3 | async-start | bytes 524288 | tf_op jit(solution)/shard_map/all_to_all | solution.py:138
  69.8 8.1 %copy-start.11 = (bf16[2,8,32,8,32]{4,3,2,1,0:T(8,128)(2,1)}, bf16[2,8,32,8,32]{4,3,2,1,0:T(8,128)(2,1)S(1)}, u32[]{:S(2)}) copy-start(bf16[2,8,32,8,32]{4,3,2,1,0:T(8,128)(2,1)S(1)} %reshape.475) | copy-start | bytes 786436
  78.8 11.8 %all-to-all-start.4 = ((bf16[8,2,2,32,128]{4,2,1,3,0:T(2,128)(2,1)}), bf16[8,2,2,32,128]{4,2,1,3,0:T(2,128)(2,1)S(1)}, u32[]{:S(2)}, u32[]{:S(2)}) async-start(bf16[8,2,2,32,128]{4,2,1,3,0:T(2,128)(2,1)} %copy.90), calls=%async_computation.4 | async-start | bytes 524288 | tf_op jit(solution)/shard_map/all_to_all | solution.py:138
  84.4 14.7 %collective-permute-start.2 = (bf16[1,48,8,128]{3,2,1,0:T(8,128)(2,1)S(1)}, bf16[1,48,8,128]{3,2,1,0:T(8,128)(2,1)S(1)}, u32[]{:S(2)}, u32[]{:S(2)}) collective-permute-start(bf16[1,48,8,128]{3,2,1,0:T(8,128)(2,1)S(1)} %get-tuple-element.24), channel_id=1, source_target_pairs={{0,1},{1,2},{2,3},{3,0},{4,5},{5,6},{6,7},{7,4},{8,9},{9,10},{10,1... | collective-permute-start | bytes 294920 | tf_op jit(solution)/shard_map/ppermute | solution.py:25
  86.5 12.6 %collective-permute-start.3 = (bf16[1,48,8,128]{3,2,1,0:T(8,128)(2,1)S(1)}, bf16[1,48,8,128]{3,2,1,0:T(8,128)(2,1)S(1)}, u32[]{:S(2)}, u32[]{:S(2)}) collective-permute-start(bf16[1,48,8,128]{3,2,1,0:T(8,128)(2,1)S(1)} %get-tuple-element.25), channel_id=1, source_target_pairs={{1,0},{2,1},{3,2},{0,3},{5,4},{6,5},{7,6},{4,7},{9,8},{10,9},{11,1... | collective-permute-start | bytes 294920 | tf_op jit(solution)/shard_map/ppermute | solution.py:27
  92.0 20.8 %all-to-all-start.5 = ((bf16[4,8,2,2,32,128]{5,1,3,2,4,0:T(8,128)(2,1)}), bf16[4,8,2,2,32,128]{5,1,3,2,4,0:T(8,128)(2,1)}, u32[]{:S(2)}, u32[]{:S(2)}) async-start(bf16[4,8,2,2,32,128]{5,1,3,2,4,0:T(8,128)(2,1)} %broadcast_in_dim.40), calls=%async_computation.5 | async-start | bytes 2097152 | tf_op jit(solution)/shard_map/all_to_all | solution.py:138
  103.7 2.7 %copy-start.6 = (bf16[3,32,64,80]{3,1,2,0:T(8,128)(2,1)S(1)}, bf16[3,32,64,80]{3,1,2,0:T(8,128)(2,1)}, u32[]{:S(2)}) copy-start(bf16[3,32,64,80]{3,1,2,0:T(8,128)(2,1)} %convolution_convert_fusion.6) | copy-start | bytes 2949124
  103.7 2.7 %copy-start.15 = (bf16[32,80,128]{2,1,0:T(8,128)(2,1)S(1)}, bf16[32,80,128]{2,1,0:T(8,128)(2,1)}, u32[]{:S(2)}) copy-start(bf16[32,80,128]{2,1,0:T(8,128)(2,1)} %gather_fusion.2) | copy-start | bytes 1966084
  106.3 6.5 %copy-start.20 = (bf16[64,2,64]{0,2,1:T(8,128)(2,1)S(1)}, bf16[64,2,64]{0,2,1:T(8,128)(2,1)}, u32[]{:S(2)}) copy-start(bf16[64,2,64]{0,2,1:T(8,128)(2,1)} %get-tuple-element.33) | copy-start | bytes 49156
  123.2 5.7 %copy-start.16 = (bf16[3,48,3,17]{3,2,0,1:T(4,128)(2,1)S(1)}, bf16[3,48,3,17]{3,2,0,1:T(4,128)(2,1)}, u32[]{:S(2)}) copy-start(bf16[3,48,3,17]{3,2,0,1:T(4,128)(2,1)} %select_bitcast_fusion) | copy-start | bytes 44068
  124.6 18.0 %all-to-all-start.6 = ((bf16[4,8,2,2,32,128]{5,4,2,1,3,0:T(8,128)(2,1)}), bf16[4,8,2,2,32,128]{5,4,2,1,3,0:T(8,128)(2,1)S(1)}, u32[]{:S(2)}, u32[]{:S(2)}) async-start(bf16[4,8,2,2,32,128]{5,4,2,1,3,0:T(8,128)(2,1)} %copy.99), calls=%async_computation.6 | async-start | bytes 2097152 | tf_op jit(solution)/shard_map/all_to_all | solution.py:138
  132.4 14.5 %copy-start.26 = (pred[48]{0:T(512)(128)(4,1)S(1)}, pred[48]{0:T(512)(128)(4,1)}, u32[]{:S(2)}) copy-start(pred[48]{0:T(512)(128)(4,1)} %copy-done.25) | copy-start | bytes 148
  134.6 19.6 %copy-start.12 = (bf16[2,8,32,8,32]{4,3,2,1,0:T(8,128)(2,1)S(1)}, bf16[2,8,32,8,32]{4,3,2,1,0:T(8,128)(2,1)}, u32[]{:S(2)}) copy-start(bf16[2,8,32,8,32]{4,3,2,1,0:T(8,128)(2,1)} %copy-done.11) | copy-start | bytes 786436
  143.5 10.7 %all-to-all-start.7 = ((bf16[8,2,2,32,128]{4,3,2,1,0:T(8,128)(2,1)}), bf16[8,2,2,32,128]{4,3,2,1,0:T(8,128)(2,1)S(1)}, u32[]{:S(2)}, u32[]{:S(2)}) async-start(bf16[8,2,2,32,128]{4,3,2,1,0:T(8,128)(2,1)} %copy.100), calls=%async_computation.7 | async-start | bytes 524288 | tf_op jit(solution)/shard_map/all_to_all | solution.py:138
  149.2 11.2 %copy-start.5 = (bf16[1,32,64,128]{3,2,1,0:T(8,128)(2,1)S(1)}, bf16[1,32,64,128]{3,2,1,0:T(8,128)(2,1)}, u32[]{:S(2)}) copy-start(bf16[1,32,64,128]{3,2,1,0:T(8,128)(2,1)} %get-tuple-element.18) | copy-start | bytes 1572868
  149.2 15.5 %copy-start.10 = (bf16[2,8,32,8,32]{4,3,2,1,0:T(8,128)(2,1)S(1)}, bf16[2,8,32,8,32]{4,3,2,1,0:T(8,128)(2,1)}, u32[]{:S(2)}) copy-start(bf16[2,8,32,8,32]{4,3,2,1,0:T(8,128)(2,1)} %reshape.476) | copy-start | bytes 786436
  155.5 18.2 %all-to-all-start.8 = ((bf16[8,32,2,2,128]{4,3,1,2,0:T(2,128)(2,1)}), bf16[8,32,2,2,128]{4,3,1,2,0:T(2,128)(2,1)S(1)}, u32[]{:S(2)}, u32[]{:S(2)}) async-start(bf16[8,32,2,2,128]{4,3,1,2,0:T(2,128)(2,1)} %copy.103), calls=%async_computation.8 | async-start | bytes 524288 | tf_op jit(solution)/shard_map/all_to_all | solution.py:138
  160.4 10.8 %collective-permute-start.4 = (bf16[1,8,64,128]{3,2,1,0:T(8,128)(2,1)S(1)}, bf16[1,8,64,128]{3,2,1,0:T(8,128)(2,1)S(1)}, u32[]{:S(2)}, u32[]{:S(2)}) collective-permute-start(bf16[1,8,64,128]{3,2,1,0:T(8,128)(2,1)S(1)} %get-tuple-element.26), channel_id=1, source_target_pairs={{0,4},{4,8},{8,12},{12,16},{16,20},{20,24},{24,28},{28,0},{1,5},{5... | collective-permute-start | bytes 393224 | tf_op jit(solution)/shard_map/ppermute | solution.py:25
  161.9 9.3 %collective-permute-start.5 = (bf16[1,8,64,128]{3,2,1,0:T(8,128)(2,1)S(1)}, bf16[1,8,64,128]{3,2,1,0:T(8,128)(2,1)S(1)}, u32[]{:S(2)}, u32[]{:S(2)}) collective-permute-start(bf16[1,8,64,128]{3,2,1,0:T(8,128)(2,1)S(1)} %get-tuple-element.27), channel_id=1, source_target_pairs={{4,0},{8,4},{12,8},{16,12},{20,16},{24,20},{28,24},{0,28},{5,1},{9... | collective-permute-start | bytes 393224 | tf_op jit(solution)/shard_map/ppermute | solution.py:27
  171.2 5.9 %copy-start.22 = (bf16[1,8,64,128]{3,2,1,0:T(8,128)(2,1)}, bf16[1,8,64,128]{3,2,1,0:T(8,128)(2,1)S(1)}, u32[]{:S(2)}) copy-start(bf16[1,8,64,128]{3,2,1,0:T(8,128)(2,1)S(1)} %collective-permute-done.5) | copy-start | bytes 393220
  171.2 10.4 %collective-permute-start.6 = (bf16[1,48,8,128]{3,2,1,0:T(8,128)(2,1)S(1)}, bf16[1,48,8,128]{3,2,1,0:T(8,128)(2,1)S(1)}, u32[]{:S(2)}, u32[]{:S(2)}) collective-permute-start(bf16[1,48,8,128]{3,2,1,0:T(8,128)(2,1)S(1)} %get-tuple-element.22), channel_id=1, source_target_pairs={{0,1},{1,2},{2,3},{3,0},{4,5},{5,6},{6,7},{7,4},{8,9},{9,10},{10,1... | collective-permute-start | bytes 294920 | tf_op jit(solution)/shard_map/ppermute | solution.py:25
  173.7 7.9 %collective-permute-start.7 = (bf16[1,48,8,128]{3,2,1,0:T(8,128)(2,1)S(1)}, bf16[1,48,8,128]{3,2,1,0:T(8,128)(2,1)}, u32[]{:S(2)}, u32[]{:S(2)}) collective-permute-start(bf16[1,48,8,128]{3,2,1,0:T(8,128)(2,1)S(1)} %get-tuple-element.23), channel_id=1, source_target_pairs={{1,0},{2,1},{3,2},{0,3},{5,4},{6,5},{7,6},{4,7},{9,8},{10,9},{11,1... | collective-permute-start | bytes 294920 | tf_op jit(solution)/shard_map/ppermute | solution.py:27
  178.0 10.5 %all-to-all-start.9 = ((bf16[8,32,2,2,128]{4,1,3,2,0:T(8,128)(2,1)}), bf16[8,32,2,2,128]{4,1,3,2,0:T(8,128)(2,1)S(1)}, u32[]{:S(2)}, u32[]{:S(2)}) async-start(bf16[8,32,2,2,128]{4,1,3,2,0:T(8,128)(2,1)} %copy.106), calls=%async_computation.9 | async-start | bytes 524288 | tf_op jit(solution)/shard_map/all_to_all | solution.py:138
  181.6 2.3 copy-start.3
  191.0 11.5 %all-to-all-start.10 = ((bf16[8,2,2,32,128]{4,2,1,3,0:T(2,128)(2,1)}), bf16[8,2,2,32,128]{4,2,1,3,0:T(2,128)(2,1)S(1)}, u32[]{:S(2)}, u32[]{:S(2)}) async-start(bf16[8,2,2,32,128]{4,2,1,3,0:T(2,128)(2,1)} %copy.109), calls=%async_computation.10 | async-start | bytes 524288 | tf_op jit(solution)/shard_map/all_to_all | solution.py:138
  195.4 4.1 %copy-start.1 = (bf16[3,48,64,80]{3,1,2,0:T(8,128)(2,1)S(1)}, bf16[3,48,64,80]{3,1,2,0:T(8,128)(2,1)}, u32[]{:S(2)}) copy-start(bf16[3,48,64,80]{3,1,2,0:T(8,128)(2,1)} %convolution_convert_fusion.3) | copy-start | bytes 4423684
  204.0 20.9 %all-to-all-start.11 = ((bf16[4,8,2,2,32,128]{5,1,3,2,4,0:T(8,128)(2,1)}), bf16[4,8,2,2,32,128]{5,1,3,2,4,0:T(8,128)(2,1)}, u32[]{:S(2)}, u32[]{:S(2)}) async-start(bf16[4,8,2,2,32,128]{5,1,3,2,4,0:T(8,128)(2,1)} %broadcast_in_dim.41), calls=%async_computation.11 | async-start | bytes 2097152 | tf_op jit(solution)/shard_map/all_to_all | solution.py:138
  211.2 4.1 %copy-start.2 = (bf16[3,48,64,80]{3,1,2,0:T(8,128)(2,1)S(1)}, bf16[3,48,64,80]{3,1,2,0:T(8,128)(2,1)}, u32[]{:S(2)}) copy-start(bf16[3,48,64,80]{3,1,2,0:T(8,128)(2,1)} %convolution_convert_fusion.1) | copy-start | bytes 4423684
  216.5 8.4 %copy-start.8 = (f32[64,128,32]{1,2,0:T(8,128)S(1)}, f32[64,128,32]{1,2,0:T(8,128)}, u32[]{:S(2)}) copy-start(f32[64,128,32]{1,2,0:T(8,128)} %fusion.18) | copy-start | bytes 3145732
  216.5 8.4 %copy-start.9 = (f32[64,128,32]{1,2,0:T(8,128)S(1)}, f32[64,128,32]{1,2,0:T(8,128)}, u32[]{:S(2)}) copy-start(f32[64,128,32]{1,2,0:T(8,128)} %fusion.20) | copy-start | bytes 3145732
  216.6 8.4 %copy-start.19 = (bf16[64,2,64]{0,2,1:T(8,128)(2,1)S(1)}, bf16[64,2,64]{0,2,1:T(8,128)(2,1)}, u32[]{:S(2)}) copy-start(bf16[64,2,64]{0,2,1:T(8,128)(2,1)} %copy-done.18) | copy-start | bytes 49156
where the time goes:
time: 231 us; the launch traced here: 229 us
  starting transfers between devices  72.4 us (31%)
  matrix products  62.7 us (27%)
  waiting for transfers between devices  45.7 us (20%)
  local copies, waits for them, and re-layouts  33.8 us (15%)
  other arithmetic  9.73 us (4%)
  Pallas kernels  3.62 us (2%)
    all_to_all x12, starting transfers between devices, swap(): return lax.all_to_all(blocks, axis, split_axis=0, concat_axis=0, tiled=True)  58.5 us
    all_to_all x12, waiting for transfers between devices, swap(): return lax.all_to_all(blocks, axis, split_axis=0, concat_axis=0, tiled=True)  42 us
    dot_general x3, matrix products, per_device(): jnp.einsum('ji,aiqc->ajqc', placing, spread, precision=lax.Precision.HIGH...  9.9 us
    ppermute x4, starting transfers between devices, extended(): lax.ppermute(tail, axis, [(i, (i + 1) % count) for i in range(count)])  8.11 us
    dot_general x3, matrix products, per_device(): jnp.einsum('kis,qts->kiqt', pad_basis[:, :, band_index, :].astype(jnp.flo...  6.66 us
    dot_general x2, matrix products, synthesis(): jnp.einsum('jbekic,fkjbe->ifc', every, dft_table, preferred_element_type=...  6.6 us
    dot_general x1, matrix products, per_device(): jnp.einsum('kaifc,kcd->aifd', local_terms, local_weight, preferred_elemen...  6.42 us
    dot_general x3, matrix products, per_device(): jnp.einsum('kiqt,kaitc->aiqc', banded, grad_local, preferred_element_type...  5.93 us
  transfers between devices with their start and end apart: 20, of which 11 were waited for; matrix products, arithmetic and copies ran while one was open for 36% of the time, Pallas kernels for 2%

commit v1 on v0

--- a/solution.py
+++ b/solution.py
@@ -1,3 +1,4 @@
+import functools
 import math
 
 import jax
@@ -134,37 +135,212 @@
     )(forward_gain, forward_gain * backward_gain, orders, trig)
 
 
-def swap(blocks, axis):
-    return lax.all_to_all(blocks, axis, split_axis=0, concat_axis=0, tiled=True)
-
-
 def margin(blocks):
     return extended(blocks, (("lat", 1), ("lon", 2)), HW)
 
 
-def analysis(field_blocks, dft_table, degree_table):
-    partial = jnp.einsum(
-        "ifc,fkjbe->jbekic", field_blocks, dft_table, preferred_element_type=jnp.float32
-    ).astype(jnp.bfloat16)
-    fourier = jnp.sum(swap(partial, "lon").astype(jnp.float32), axis=0).astype(jnp.bfloat16)
-    columns = swap(fourier, "lat")
-    degrees = jnp.einsum(
-        "sekic,edlsi->dlekc", columns, degree_table, preferred_element_type=jnp.float32
-    ).astype(jnp.bfloat16)
-    return swap(degrees, "lat")
-
-
-def synthesis(spectrum, degree_table, dft_table):
-    by_degree = swap(spectrum, "lat")
-    zonal_modes = jnp.einsum(
-        "dlekc,edlsi->sekic", by_degree, degree_table, preferred_element_type=jnp.float32
-    ).astype(jnp.bfloat16)
-    by_order = swap(zonal_modes, "lat")
-    lon_count = dft_table.shape[2]
-    every = swap(jnp.broadcast_to(by_order[None], (lon_count,) + by_order.shape), "lon")
-    return jnp.einsum(
-        "jbekic,fkjbe->ifc", every, dft_table, preferred_element_type=jnp.float32
-    ).astype(jnp.bfloat16)
+def spectral_kernel(
+    lat_count,
+    lon_count,
+    data_ref,
+    first_ref,
+    down_ref,
+    up_ref,
+    last_ref,
+    mix_ref,
+    out_ref,
+    part_out,
+    part_in,
+    rows_out,
+    rows_in,
+    deg_out,
+    deg_in,
+    mixed_out,
+    mixed_in,
+    zonal_out,
+    zonal_in,
+    grid_out,
+    grid_in,
+    turned,
+    blended,
+    lon_send,
+    lon_recv,
+    lat_send,
+    lat_recv,
+):
+    row_count, lon_dev, channels = data_ref.shape
+    order_share = down_ref.shape[0]
+    degree_dev = mix_ref.shape[0]
+    wide = 2 * channels
+    share = lat_count * order_share
+    modes = 2 * share
+    lat_me = lax.axis_index("lat")
+    lon_me = lax.axis_index("lon")
+
+    def others(me, count):
+        return [lax.rem(me + step, count) for step in range(1, count)]
+
+    barrier = pltpu.get_barrier_semaphore()
+    for axis, me, count in (("lat", lat_me, lat_count), ("lon", lon_me, lon_count)):
+        for peer in others(me, count):
+            pl.semaphore_signal(
+                barrier, inc=1, device_id={axis: peer}, device_id_type=pl.DeviceIdType.MESH
+            )
+
+    def exchange(axis, number, source, target, whole):
+        me, count, send, recv = (
+            (lat_me, lat_count, lat_send, lat_recv)
+            if axis == "lat"
+            else (lon_me, lon_count, lon_send, lon_recv)
+        )
+        copies = []
+        for peer in others(me, count):
+            copy = pltpu.make_async_remote_copy(
+                src_ref=source if whole else source.at[peer],
+                dst_ref=target.at[me],
+                send_sem=send.at[number, peer],
+                recv_sem=recv.at[number, me],
+                device_id={axis: peer},
+                device_id_type=pl.DeviceIdType.MESH,
+            )
+            copy.start()
+            copies.append(copy)
+        target[me] = source[...] if whole else source[me]
+        for peer in others(me, count):
+            pltpu.make_async_remote_copy(
+                src_ref=source if whole else source.at[peer],
+                dst_ref=target.at[peer],
+                send_sem=send.at[number, peer],
+                recv_sem=recv.at[number, peer],
+                device_id={axis: peer},
+                device_id_type=pl.DeviceIdType.MESH,
+            ).wait_recv()
+        for copy in copies:
+            copy.wait_send()
+
+    group = 8
+
+    def transform(index, carry):
+        for step in range(group):
+            row = index * group + step
+            part = jnp.dot(first_ref[...], data_ref[row], preferred_element_type=jnp.float32)
+            part_out[:, row] = part.astype(jnp.bfloat16).reshape(lon_count, modes, channels)
+        return carry
+
+    lax.fori_loop(0, row_count // group, transform, 0)
+    pl.semaphore_wait(barrier, lat_count + lon_count - 2)
+    exchange("lon", 0, part_out, part_in, False)
+
+    total = part_in[0].astype(jnp.float32)
+    for sector in range(1, lon_count):
+        total = total + part_in[sector].astype(jnp.float32)
+    rows_out[...] = (
+        jnp.swapaxes(total, 0, 1)
+        .astype(jnp.bfloat16)
+        .reshape(lat_count, order_share, 2, row_count, channels)
+    )
+    exchange("lat", 0, rows_out, rows_in, False)
+
+    for e in range(order_share):
+        columns = jnp.concatenate(
+            [rows_in[:, e, part].reshape(lat_count * row_count, channels) for part in range(2)],
+            axis=1,
+        )
+        degrees = jnp.dot(down_ref[e], columns, preferred_element_type=jnp.float32)
+        deg_out[:, e] = degrees.astype(jnp.bfloat16).reshape(lat_count, degree_dev, wide)
+    exchange("lat", 1, deg_out, deg_in, False)
+
+    by_degree = deg_in[...].reshape(share, degree_dev, wide).astype(jnp.float32)
+    turned[...] = jnp.swapaxes(by_degree, 0, 1).astype(jnp.bfloat16)
+
+    def blend(index, carry):
+        for step in range(group):
+            degree = index * group + step
+            pair = jnp.concatenate(
+                [turned[degree, :, :channels], turned[degree, :, channels:]], axis=0
+            )
+            weights = jnp.concatenate([mix_ref[degree, 0], mix_ref[degree, 1]], axis=1)
+            product = jnp.dot(pair, weights, preferred_element_type=jnp.float32)
+            blended[degree, :, :channels] = product[:share, :channels] - product[share:, channels:]
+            blended[degree, :, channels:] = product[:share, channels:] + product[share:, :channels]
+        return carry
+
+    lax.fori_loop(0, degree_dev // group, blend, 0)
+    mixed_out[...] = (
+        jnp.swapaxes(blended[...], 0, 1)
+        .astype(jnp.bfloat16)
+        .reshape(lat_count, order_share, degree_dev, wide)
+    )
+    exchange("lat", 2, mixed_out, mixed_in, False)
+
+    for e in range(order_share):
+        spectrum = mixed_in[:, e].reshape(lat_count * degree_dev, wide)
+        zonal = lax.dot_general(
+            up_ref[e], spectrum, (((0,), (0,)), ((), ())), preferred_element_type=jnp.float32
+        ).astype(jnp.bfloat16)
+        for part in range(2):
+            zonal_out[:, e, part] = zonal[:, part * channels : (part + 1) * channels].reshape(
+                lat_count, row_count, channels
+            )
+    exchange("lat", 3, zonal_out, zonal_in, False)
+
+    by_order = zonal_in[...].reshape(modes, row_count, channels).astype(jnp.float32)
+    grid_out[...] = jnp.swapaxes(by_order, 0, 1).astype(jnp.bfloat16)
+    exchange("lon", 1, grid_out, grid_in, True)
+
+    def restore(index, carry):
+        for step in range(group):
+            row = index * group + step
+            every = grid_in[:, row].reshape(lon_count * modes, channels)
+            out_ref[row] = jnp.dot(
+                last_ref[...], every, preferred_element_type=jnp.float32
+            ).astype(jnp.bfloat16)
+        return carry
+
+    lax.fori_loop(0, row_count // group, restore, 0)
+
+
+def spectral_pass(lat_count, lon_count, data, first, down, up, last, mix):
+    row_count, lon_dev, channels = data.shape
+    order_share = down.shape[0]
+    degree_dev = mix.shape[0]
+    share = lat_count * order_share
+    wide = 2 * channels
+    bf16 = jnp.bfloat16
+    part = pltpu.VMEM((lon_count, row_count, 2 * share, channels), bf16)
+    rows = pltpu.VMEM((lat_count, order_share, 2, row_count, channels), bf16)
+    degrees = pltpu.VMEM((lat_count, order_share, degree_dev, wide), bf16)
+    vmem = pl.BlockSpec(memory_space=pltpu.VMEM)
+    return pl.pallas_call(
+        functools.partial(spectral_kernel, lat_count, lon_count),
+        out_shape=jax.ShapeDtypeStruct(data.shape, bf16),
+        in_specs=[vmem] * 6,
+        out_specs=vmem,
+        scratch_shapes=[
+            part,
+            part,
+            rows,
+            rows,
+            degrees,
+            degrees,
+            degrees,
+            degrees,
+            rows,
+            rows,
+            pltpu.VMEM((row_count, 2 * share, channels), bf16),
+            part,
+            pltpu.VMEM((degree_dev, share, wide), bf16),
+            pltpu.VMEM((degree_dev, share, wide), jnp.float32),
+            pltpu.SemaphoreType.DMA((2, lon_count)),
+            pltpu.SemaphoreType.DMA((2, lon_count)),
+            pltpu.SemaphoreType.DMA((4, lat_count)),
+            pltpu.SemaphoreType.DMA((4, lat_count)),
+        ],
+        compiler_params=pltpu.CompilerParams(
+            collective_id=0, has_side_effects=True, vmem_limit_bytes=48 * 1024 * 1024
+        ),
+        name="spectral_pass",
+    )(data, first, down, up, last, mix)
 
 
 def per_device(fields, cotangent, spectral_weight, local_weight, filter_basis, neighbor_rows):
@@ -186,26 +362,15 @@
     table_shape = (lon_dev, 2, lon_count, lat_count, order_share)
     to_modes = lax.dynamic_slice_in_dim(to_modes, lon_index * lon_dev, lon_dev, 0)
     from_modes = lax.dynamic_slice_in_dim(from_modes, lon_index * lon_dev, lon_dev, 0)
-    to_modes = to_modes.reshape(table_shape)
-    from_modes = from_modes.reshape(table_shape)
+    to_modes = to_modes.reshape(table_shape).transpose(0, 2, 3, 4, 1).reshape(lon_dev, -1)
+    from_modes = from_modes.reshape(table_shape).transpose(0, 2, 3, 4, 1).reshape(lon_dev, -1)
     orders = (
         lon_index * mode_dev + lat_index * order_share + jnp.arange(order_share, dtype=jnp.int32)
     )
     weighted, unweighted = legendre_tables(orders, degree_dev * lat_count, total_lat)
-    degree_shape = (order_share, lat_count, degree_dev, lat_count, lat_dev)
-    weighted = weighted.reshape(degree_shape)
-    unweighted = unweighted.reshape(degree_shape)
-    real_part = spectral_weight[:, 0]
-    imag_part = spectral_weight[:, 1]
-    complex_mix = jnp.stack(
-        [jnp.stack([real_part, imag_part], axis=2), jnp.stack([-imag_part, real_part], axis=2)],
-        axis=1,
-    )
-    harmonics = analysis(fields[0], to_modes, weighted)
-    filtered = jnp.einsum(
-        "bdekc,dkcjx->bdejx", harmonics, complex_mix, preferred_element_type=jnp.float32
-    ).astype(jnp.bfloat16)
-    spectral = synthesis(filtered, unweighted, from_modes)[None]
+    spectral = spectral_pass(
+        lat_count, lon_count, fields[0], to_modes.T, weighted, unweighted, from_modes, spectral_weight
+    )[None]
     padded = margin(fields)
     row_base = lat_index * lat_dev
     my_rows = lax.dynamic_slice_in_dim(neighbor_rows, row_base, lat_dev, 0)
@@ -232,11 +397,12 @@
     activation, derivative = gelu_parts(pre_act)
     block_output = (fields.astype(jnp.float32) + activation).astype(jnp.bfloat16)
     grad_mix = (cotangent.astype(jnp.float32) * derivative).astype(jnp.bfloat16)
-    grad_filtered = analysis(grad_mix[0], from_modes, unweighted)
-    grad_harmonics = jnp.einsum(
-        "bdejx,dkcjx->bdekc", grad_filtered, complex_mix, preferred_element_type=jnp.float32
-    ).astype(jnp.bfloat16)
-    grad_spectral = synthesis(grad_harmonics, weighted, to_modes)[None]
+    adjoint_mix = jnp.stack(
+        [spectral_weight[:, 0].transpose(0, 2, 1), -spectral_weight[:, 1].transpose(0, 2, 1)], axis=1
+    )
+    grad_spectral = spectral_pass(
+        lat_count, lon_count, grad_mix[0], from_modes.T, unweighted, weighted, to_modes, adjoint_mix
+    )[None]
     grad_padded = margin(grad_mix)
     grad_local = jnp.einsum(
         "aitd,kcd->kaitc", grad_padded, local_weight, preferred_element_type=jnp.float32

time: 231 us -> 216 us (0.935)
  Pallas kernels: 3.62 us -> 116 us
  starting transfers between devices: 72.4 us -> 11.4 us
  waiting for transfers between devices: 45.7 us -> 7.85 us
  matrix products: 62.7 us -> 36.3 us
  local copies, waits for them, and re-layouts: 33.8 us -> 25.9 us
  other arithmetic: 9.73 us -> 14.6 us
    pallas_call x0 -> x2, Pallas kernels: none -> 112 us  [spectral_pass(): pl.pallas_call(functools.partial(spectral_kernel, lat_count, lon_count),...]
    all_to_all x12 -> x0, starting transfers between devices: 58.5 us -> none  [swap(): return lax.all_to_all(blocks, axis, split_axis=0, concat_axis=0, tiled=True)]
    all_to_all x12 -> x0, waiting for transfers between devices: 42 us -> none  [swap(): return lax.all_to_all(blocks, axis, split_axis=0, concat_axis=0, tiled=True)]
    dot_general x10 -> x0, matrix products: 21 us -> none  [the longest x2 6.6 us: synthesis(): jnp.einsum('jbekic,fkjbe->ifc', every, dft_table, preferred_element_type=...]
    unnamed x58 -> x64, local copies, waits for them, and re-layouts: 2.47 us -> 11.5 us
    convert_element_type x8 -> x0, local copies, waits for them, and re-layouts: 7.95 us -> none  [the longest x2 2.61 us: analysis(): partial = jnp.einsum('ifc,fkjbe->jbekic', field_blocks, dft_table, prefer...]
    reshape x4 -> x2, local copies, waits for them, and re-layouts: 7.66 us -> 0.17 us  [the longest x1 0.08 us: per_device(): from_modes.reshape(table_shape).transpose(0, 2, 3, 4, 1)]
    ppermute x4, waiting for transfers between devices: 0.01 us -> 5.23 us  [extended(): lax.ppermute(head, axis, [((i + 1) % count, i) for i in range(count)])]
  transfers between devices with their start and end apart: 20 -> 8, of which waited for: 11 -> 4; matrix products, arithmetic and copies ran while one was open for 36% -> 18% of each run, Pallas kernels for 2% -> 54%
where the time goes in v1:
time: 216 us; the launch traced here: 213 us
  Pallas kernels  116 us (54%)
  matrix products  36.3 us (17%)
  local copies, waits for them, and re-layouts  25.9 us (12%)
  other arithmetic  14.6 us (7%)
  starting transfers between devices  11.4 us (5%)
  waiting for transfers between devices  7.85 us (4%)
    pallas_call x2, Pallas kernels, spectral_pass(): pl.pallas_call(functools.partial(spectral_kernel, lat_count, lon_count),...  112 us
    unnamed x64, local copies, waits for them, and re-layouts  11.5 us
    dot_general x2, matrix products, per_device(): jnp.einsum('kift,aitc->kaifc', banded, sources, preferred_element_type=jn...  6.88 us
    dot_general x3, matrix products, per_device(): jnp.einsum('kis,qts->kiqt', pad_basis[:, :, band_index, :].astype(jnp.flo...  6.77 us
    dot_general x1, matrix products, per_device(): jnp.einsum('kaifc,kcd->aifd', local_terms, local_weight, preferred_elemen...  6.7 us
    ppermute x4, starting transfers between devices, extended(): lax.ppermute(tail, axis, [(i, (i + 1) % count) for i in range(count)])  5.89 us
    ppermute x4, starting transfers between devices, extended(): lax.ppermute(head, axis, [((i + 1) % count, i) for i in range(count)])  5.47 us
    dot_general x3, matrix products, per_device(): jnp.einsum('kis,fts->kift', my_basis[:, :, band_index, :].astype(jnp.floa...  5.36 us
  transfers between devices with their start and end apart: 8, of which 4 were waited for; matrix products, arithmetic and copies ran while one was open for 18% of the time, Pallas kernels for 54%

profile of v1, /device:TPU:1, one launch (start us, length us, event | category | flops | bytes accessed | tf_op | source)
XLA Modules:
  0.0 213.2 jit_solution(15376837407613001424)
XLA Ops:
  0.6 1.7 fusion.144
  2.4 2.1 collective-permute-start
  4.4 3.0 %collective-permute-start.1 = (bf16[1,8,64,128]{3,2,1,0:T(8,128)(2,1)}, bf16[1,8,64,128]{3,2,1,0:T(8,128)(2,1)}, u32[]{:S(2)}, u32[]{:S(2)}) collective-permute-start(bf16[1,8,64,128]{3,2,1,0:T(8,128)(2,1)} %get-tuple-element.26), channel_id=1, source_target_pairs={{4,0},{8,4},{12,8},{16,12},{20,16},{24,20},{28,24},{0,28},{5,1},{9... | collective-permute-start | bytes 393224 | tf_op jit(solution)/shard_map/ppermute | solution.py:28
  7.5 0.6 add_multiply_fusion.2
  8.1 0.5 iota_add_fusion.1
  8.6 0.6 sine_log_fusion
  9.2 0.6 sine_multiply_fusion
  10.2 0.6 compare_select_fusion.7
  10.8 0.6 fusion.134
  11.4 0.5 compare_and_fusion.4
  11.9 0.8 copy.102
  12.7 0.8 constant_dynamic-slice_fusion.2
  13.5 0.6 compare_and_fusion
  14.2 2.1 copy.99
  16.3 1.1 constant_dynamic-slice_fusion.3
  17.4 1.8 convolution_convert_fusion.5
  19.2 1.8 convolution_convert_fusion.6
  21.0 1.8 convolution_convert_fusion.4
  22.8 1.5 fusion.141
  24.3 1.6 copy.132
  25.9 1.1 negate_bitcast_fusion
  27.0 1.9 gather_fusion
  28.9 0.7 select_bitcast_fusion
  30.0 0.6 gather_fusion.1
  30.6 0.7 broadcast_select_fusion
  31.3 2.2 %convolution_convert_fusion.2 = bf16[3,48,64,80]{3,1,2,0:T(8,128)(2,1)} fusion(s32[64,80]{1,0:T(8,128)S(1)} %subtract_add_fusion, bf16[3,48,1,17]{1,3,2,0:T(8,128)(2,1)S(1)} %copy.104), kind=kOutput, calls=%fused_computation.18 | convolution fusion | flops 25891840 | bytes 1499936 | tf_op jit(solution)/shard_map/kis,qts->kiqt/dot_general | solution.py:420
  33.6 2.3 %convolution_convert_fusion.3 = bf16[3,48,64,80]{3,1,2,0:T(8,128)(2,1)} fusion(s32[64,80]{1,0:T(8,128)S(1)} %subtract_add_fusion, bf16[3,48,1,17]{1,3,2,0:T(8,128)(2,1)S(1)} %copy.100), kind=kOutput, calls=%fused_computation.19 | convolution fusion | flops 25891840 | bytes 1499936 | tf_op jit(solution)/shard_map/kis,qts->kiqt/dot_general | solution.py:420
  36.0 2.3 %convolution_convert_fusion.1 = bf16[3,48,64,80]{3,1,2,0:T(8,128)(2,1)} fusion(s32[64,80]{1,0:T(8,128)S(1)} %subtract_add_fusion, bf16[3,48,1,17]{1,3,2,0:T(8,128)(2,1)S(1)} %copy.109), kind=kOutput, calls=%fused_computation.17 | convolution fusion | flops 25891840 | bytes 1499936 | tf_op jit(solution)/shard_map/kis,qts->kiqt/dot_general | solution.py:420
  38.5 0.7 sqrt_multiply_fusion
  39.2 0.6 pad_maximum_fusion.4.trig_ref
  39.9 2.3 %copy.131 = bf16[32,1,128,128]{2,3,0,1:T(8,128)(2,1)} copy(bf16[32,1,128,128]{3,2,1,0:T(8,128)(2,1)} %get-tuple-element.16) | data formatting | bytes 2097152
  42.2 3.8 %legendre_tables.1 = (bf16[2,256,256]{2,1,0:T(8,128)(2,1)}, bf16[2,256,256]{2,1,0:T(8,128)(2,1)}) custom-call(f32[2,256]{1,0:T(2,128)} %get-tuple-element.37.gain_ref, f32[2,256]{1,0:T(2,128)} %get-tuple-element.36.back_ref, s32[2]{0:T(128)} %get-tuple-element.48.orders_ref, f32[4,256]{1,0:T(4,128)} %pad_maximum_fusion.4.trig_ref), custom_call_target="tpu_custom_call" | custom-call | tf_op jit(solution)/shard_map/legendre_tables/pallas_call | solution.py:129
  46.0 0.9 copy-done.3
  46.9 0.9 copy-done.5
  47.9 56.8 %spectral_pass.2 = bf16[32,64,128]{2,1,0:T(8,128)(2,1)S(1)} custom-call(bf16[32,64,128]{2,1,0:T(8,128)(2,1)S(1)} %bitcast.229, bf16[128,64]{1,0:T(8,128)(2,1)S(1)} %bitcast.233, bf16[2,256,256]{2,1,0:T(8,128)(2,1)S(1)} %copy-done.3, bf16[2,256,256]{2,1,0:T(8,128)(2,1)S(1)} %copy-done.5, bf16[64,128]{1,0:T(8,128)(2,1)S(1)} %copy.88.last_ref, ...), custom_call_target="tpu_custom_call" | custom-call | tf_op jit(solution)/shard_map/spectral_pass/pallas_call | solution.py:314
  104.7 0.8 copy-done.7
  105.5 0.9 constant_dynamic-update-slice_fusion.2
  106.5 0.9 constant_dynamic-update-slice_fusion
  107.5 0.5 collective-permute-start.3
  108.1 1.5 collective-permute-done.2
  109.5 2.3 %collective-permute-done.3 = bf16[1,48,8,128]{3,2,1,0:T(8,128)(2,1)S(1)} collective-permute-done((bf16[1,48,8,128]{3,2,1,0:T(8,128)(2,1)S(1)}, bf16[1,48,8,128]{3,2,1,0:T(8,128)(2,1)S(1)}, u32[]{:S(2)}, u32[]{:S(2)}) %collective-permute-start.3) | collective-permute-done | bytes 98336 | tf_op jit(solution)/shard_map/ppermute | solution.py:28
  111.9 1.5 gather_fusion.3
  113.4 1.5 gather_fusion.2
  114.9 1.5 gather_fusion.4
  116.4 4.3 %fusion.18 = f32[32,128,3,64]{1,3,2,0:T(8,128)} fusion(bf16[3,32,64,80]{3,1,2,0:T(8,128)(2,1)} %convolution_convert_fusion.5, bf16[32,80,128]{2,1,0:T(8,128)(2,1)} %gather_fusion.3, pred[32]{0:T(512)(128)(4,1)S(1)} %copy-done.18), kind=kOutput, calls=%fused_computation.32 | convolution fusion | flops 126156800 | bytes 4784160 | tf_op jit(solution)/shard_map/kift,aitc->kaifc/dot_general | solution.py:390
  120.7 2.6 %fusion.20 = f32[32,128,3,64]{1,3,2,0:T(8,128)} fusion(bf16[3,32,64,80]{3,1,2,0:T(8,128)(2,1)S(1)} %copy-done.12, bf16[32,80,128]{2,1,0:T(8,128)(2,1)S(1)} %copy-done.13, pred[32]{0:T(512)(128)(4,1)S(1)} %copy-done.17), kind=kOutput, calls=%fused_computation.34 | convolution fusion | flops 126156800 | bytes 4784160 | tf_op jit(solution)/shard_map/kift,aitc->kaifc/dot_general | solution.py:390
  123.3 6.7 %fusion.51 = (bf16[1,32,64,128]{3,2,1,0:T(8,128)(2,1)S(1)}, bf16[1,32,64,128]{3,2,1,0:T(8,128)(2,1)}) fusion(bf16[1,32,64,128]{3,2,1,0:T(8,128)(2,1)} %param.9, bf16[1,32,64,128]{3,2,1,0:T(8,128)(2,1)S(1)} %copy-done.2, bf16[3,128,128]{2,1,0:T(8,128)(2,1)S(1)} %copy-done, bf16[3,32,64,80]{3,1,2,0:T(8,128)(2,1)} %convolution_convert_fusion.4, ...), kind=kOutput, calls=%fused_computation.45 | convolution fusion | flops 336658432 | bytes 10649632 | tf_op jit(solution)/shard_map/kaifc,kcd->aifd/dot_general | solution.py:394
  130.0 0.7 fusion.143
  130.7 2.2 %collective-permute-start.4 = (bf16[1,8,64,128]{3,2,1,0:T(8,128)(2,1)}, bf16[1,8,64,128]{3,2,1,0:T(8,128)(2,1)S(1)}, u32[]{:S(2)}, u32[]{:S(2)}) collective-permute-start(bf16[1,8,64,128]{3,2,1,0:T(8,128)(2,1)} %get-tuple-element.24), channel_id=1, source_target_pairs={{0,4},{4,8},{8,12},{12,16},{16,20},{20,24},{24,28},{28,0},{1,5},{5... | collective-permute-start | bytes 393224 | tf_op jit(solution)/shard_map/ppermute | solution.py:26
  132.9 1.9 collective-permute-start.5
  134.9 1.8 pad_maximum_fusion.mix_ref
  137.0 1.2 collective-permute-done.4
  138.1 2.9 %collective-permute-done.5 = bf16[1,8,64,128]{3,2,1,0:T(8,128)(2,1)} collective-permute-done((bf16[1,8,64,128]{3,2,1,0:T(8,128)(2,1)}, bf16[1,8,64,128]{3,2,1,0:T(8,128)(2,1)}, u32[]{:S(2)}, u32[]{:S(2)}) %collective-permute-start.5) | collective-permute-done | bytes 131104 | tf_op jit(solution)/shard_map/ppermute | solution.py:28
  141.0 0.8 pad_maximum_fusion.3
  141.8 1.5 collective-permute-start.6
  143.4 55.6 %spectral_pass.3 = bf16[32,64,128]{2,1,0:T(8,128)(2,1)S(1)} custom-call(bf16[32,64,128]{2,1,0:T(8,128)(2,1)S(1)} %bitcast.230, bf16[128,64]{1,0:T(8,128)(2,1)S(1)} %bitcast.232, bf16[2,256,256]{2,1,0:T(8,128)(2,1)S(1)} %copy-done.6, bf16[2,256,256]{2,1,0:T(8,128)(2,1)S(1)} %copy-done.4, bf16[64,128]{1,0:T(8,128)(2,1)S(1)} %copy.98.last_ref, ...), custom_call_target="tpu_custom_call" | custom-call | tf_op jit(solution)/shard_map/spectral_pass/pallas_call | solution.py:314
  199.0 2.0 convolution_convert_fusion
  201.0 1.2 fusion.31
  202.6 1.2 fusion.36
  204.3 1.2 fusion.26
  205.5 1.7 fusion.13
  207.2 1.7 fusion.15
  208.9 1.7 fusion.11
  210.5 2.6 %fusion.53 = bf16[1,32,64,128]{3,2,1,0:T(8,128)(2,1)} fusion(bf16[1,32,64,128]{3,2,1,0:T(8,128)(2,1)S(1)} %copy-done.14, f32[64,128,32]{1,2,0:T(8,128)S(1)} %fusion.11, f32[64,128,32]{1,2,0:T(8,128)S(1)} %fusion.13, f32[64,128,32]{1,2,0:T(8,128)S(1)} %fusion.15, bf16[32,64,128]{2,1,0:T(8,128)(2,1)S(1)} %spectral_pass.3), kind=kLoop, calls=%fused_computation.47 | loop fusion | flops 1835008 | bytes 4718592 | tf_op jit(solution)/shard_map/convert_element_type | solution.py:434
  (85 shorter events, 2.8 us)
Async XLA Ops:
  0.6 122.7 %copy-start = (bf16[3,128,128]{2,1,0:T(8,128)(2,1)S(1)}, bf16[3,128,128]{2,1,0:T(8,128)(2,1)}, u32[]{:S(2)}) copy-start(bf16[3,128,128]{2,1,0:T(8,128)(2,1)} %param.11) | copy-start | bytes 294916
  2.4 103.1 %collective-permute-start = (bf16[1,8,64,128]{3,2,1,0:T(8,128)(2,1)}, bf16[1,8,64,128]{3,2,1,0:T(8,128)(2,1)}, u32[]{:S(2)}, u32[]{:S(2)}) collective-permute-start(bf16[1,8,64,128]{3,2,1,0:T(8,128)(2,1)} %get-tuple-element.27), channel_id=1, source_target_pairs={{0,4},{4,8},{8,12},{12,16},{16,20},{20,24},{24,28},{28,0},{1,5},{5... | collective-permute-start | bytes 393224 | tf_op jit(solution)/shard_map/ppermute | solution.py:26
  4.4 102.1 %collective-permute-start.1 = (bf16[1,8,64,128]{3,2,1,0:T(8,128)(2,1)}, bf16[1,8,64,128]{3,2,1,0:T(8,128)(2,1)}, u32[]{:S(2)}, u32[]{:S(2)}) collective-permute-start(bf16[1,8,64,128]{3,2,1,0:T(8,128)(2,1)} %get-tuple-element.26), channel_id=1, source_target_pairs={{4,0},{8,4},{12,8},{16,12},{20,16},{24,20},{28,24},{0,28},{5,1},{9... | collective-permute-start | bytes 393224 | tf_op jit(solution)/shard_map/ppermute | solution.py:28
  19.2 3.6 %copy-start.1 = (bf16[32,2,128,128]{3,2,1,0:T(8,128)(2,1)S(1)}, bf16[32,2,128,128]{3,2,1,0:T(8,128)(2,1)}, u32[]{:S(2)}) copy-start(bf16[32,2,128,128]{3,2,1,0:T(8,128)(2,1)} %mix_ref.1) | copy-start | bytes 6291460
  25.9 1.1 copy-start.26
  33.5 4.7 %copy-start.22 = (f32[256]{0:T(256)S(1)}, f32[256]{0:T(256)}, u32[]{:S(2)}) copy-start(f32[256]{0:T(256)} %sine_log_fusion) | copy-start | bytes 3076
  33.5 4.7 %copy-start.27 = (f32[2]{0:T(128)S(1)}, f32[2]{0:T(128)}, u32[]{:S(2)}) copy-start(f32[2]{0:T(128)} %get-tuple-element.46) | copy-start | bytes 28
  33.5 4.7 %copy-start.28 = (f32[2]{0:T(128)S(1)}, f32[2]{0:T(128)}, u32[]{:S(2)}) copy-start(f32[2]{0:T(128)} %get-tuple-element.49) | copy-start | bytes 28
  33.5 4.8 %copy-start.23 = (f32[64]{0:T(128)S(1)}, f32[64]{0:T(128)}, u32[]{:S(2)}) copy-start(f32[64]{0:T(128)} %compare_select_fusion.7) | copy-start | bytes 772
  33.5 4.9 %copy-start.25 = (f32[2]{0:T(128)S(1)}, f32[2]{0:T(128)}, u32[]{:S(2)}) copy-start(f32[2]{0:T(128)} %get-tuple-element.47) | copy-start | bytes 28
  33.5 5.6 %copy-start.15 = (f32[1,256]{1,0:T(1,128)S(1)}, f32[1,256]{1,0:T(1,128)}, u32[]{:S(2)}) copy-start(f32[1,256]{1,0:T(1,128)} %get-tuple-element.54) | copy-start | bytes 3076
  33.6 5.6 %copy-start.16 = (f32[1,256]{1,0:T(1,128)S(1)}, f32[1,256]{1,0:T(1,128)}, u32[]{:S(2)}) copy-start(f32[1,256]{1,0:T(1,128)} %get-tuple-element.55) | copy-start | bytes 3076
  36.0 10.0 %copy-start.2 = (bf16[1,32,64,128]{3,2,1,0:T(8,128)(2,1)S(1)}, bf16[1,32,64,128]{3,2,1,0:T(8,128)(2,1)}, u32[]{:S(2)}) copy-start(bf16[1,32,64,128]{3,2,1,0:T(8,128)(2,1)} %param.8) | copy-start | bytes 1572868
  42.2 63.3 %copy-start.20 = (s32[32]{0:T(128)S(1)}, s32[32]{0:T(128)}, u32[]{:S(2)}) copy-start(s32[32]{0:T(128)} %get-tuple-element.11) | copy-start | bytes 388
  42.2 63.3 %copy-start.21 = (s32[32]{0:T(128)S(1)}, s32[32]{0:T(128)}, u32[]{:S(2)}) copy-start(s32[32]{0:T(128)} %get-tuple-element.39) | copy-start | bytes 388
  46.0 1.0 copy-start.3
  46.9 0.9 copy-start.5
  47.9 60.2 %copy-start.19 = (s32[32]{0:T(128)S(1)}, s32[32]{0:T(128)}, u32[]{:S(2)}) copy-start(s32[32]{0:T(128)} %get-tuple-element.41) | copy-start | bytes 388
  104.7 0.8 copy-start.7
  107.5 2.0 collective-permute-start.2
  107.5 4.3 %collective-permute-start.3 = (bf16[1,48,8,128]{3,2,1,0:T(8,128)(2,1)S(1)}, bf16[1,48,8,128]{3,2,1,0:T(8,128)(2,1)S(1)}, u32[]{:S(2)}, u32[]{:S(2)}) collective-permute-start(bf16[1,48,8,128]{3,2,1,0:T(8,128)(2,1)S(1)} %get-tuple-element.23), channel_id=1, source_target_pairs={{1,0},{2,1},{3,2},{0,3},{5,4},{6,5},{7,6},{4,7},{9,8},{10,9},{11,1... | collective-permute-start | bytes 294920 | tf_op jit(solution)/shard_map/ppermute | solution.py:28
  111.9 4.4 %copy-start.18 = (pred[32]{0:T(512)(128)(4,1)S(1)}, pred[32]{0:T(512)(128)(4,1)}, u32[]{:S(2)}) copy-start(pred[32]{0:T(512)(128)(4,1)} %get-tuple-element.38) | copy-start | bytes 100
  116.4 4.3 %copy-start.12 = (bf16[3,32,64,80]{3,1,2,0:T(8,128)(2,1)S(1)}, bf16[3,32,64,80]{3,1,2,0:T(8,128)(2,1)}, u32[]{:S(2)}) copy-start(bf16[3,32,64,80]{3,1,2,0:T(8,128)(2,1)} %convolution_convert_fusion.6) | copy-start | bytes 2949124
  116.4 4.3 %copy-start.13 = (bf16[32,80,128]{2,1,0:T(8,128)(2,1)S(1)}, bf16[32,80,128]{2,1,0:T(8,128)(2,1)}, u32[]{:S(2)}) copy-start(bf16[32,80,128]{2,1,0:T(8,128)(2,1)} %gather_fusion.2) | copy-start | bytes 1966084
  116.4 4.3 %copy-start.17 = (pred[32]{0:T(512)(128)(4,1)S(1)}, pred[32]{0:T(512)(128)(4,1)}, u32[]{:S(2)}) copy-start(pred[32]{0:T(512)(128)(4,1)} %get-tuple-element.40) | copy-start | bytes 100
  120.7 2.6 %copy-start.8 = (bf16[32,64,128]{2,1,0:T(8,128)(2,1)S(1)}, bf16[32,64,128]{2,1,0:T(8,128)(2,1)}, u32[]{:S(2)}) copy-start(bf16[32,64,128]{2,1,0:T(8,128)(2,1)} %copy-done.7) | copy-start | bytes 1572868
  120.7 2.6 %copy-start.24 = (pred[32]{0:T(512)(128)(4,1)S(1)}, pred[32]{0:T(512)(128)(4,1)}, u32[]{:S(2)}) copy-start(pred[32]{0:T(512)(128)(4,1)} %get-tuple-element.10) | copy-start | bytes 100
  130.7 7.4 %collective-permute-start.4 = (bf16[1,8,64,128]{3,2,1,0:T(8,128)(2,1)}, bf16[1,8,64,128]{3,2,1,0:T(8,128)(2,1)S(1)}, u32[]{:S(2)}, u32[]{:S(2)}) collective-permute-start(bf16[1,8,64,128]{3,2,1,0:T(8,128)(2,1)} %get-tuple-element.24), channel_id=1, source_target_pairs={{0,4},{4,8},{8,12},{12,16},{16,20},{20,24},{24,28},{28,0},{1,5},{5... | collective-permute-start | bytes 393224 | tf_op jit(solution)/shard_map/ppermute | solution.py:26
  132.9 8.1 %collective-permute-start.5 = (bf16[1,8,64,128]{3,2,1,0:T(8,128)(2,1)}, bf16[1,8,64,128]{3,2,1,0:T(8,128)(2,1)}, u32[]{:S(2)}, u32[]{:S(2)}) collective-permute-start(bf16[1,8,64,128]{3,2,1,0:T(8,128)(2,1)} %get-tuple-element.25), channel_id=1, source_target_pairs={{4,0},{8,4},{12,8},{16,12},{20,16},{24,20},{28,24},{0,28},{5,1},{9... | collective-permute-start | bytes 393224 | tf_op jit(solution)/shard_map/ppermute | solution.py:28
  134.9 8.5 %copy-start.4 = (bf16[2,256,256]{2,1,0:T(8,128)(2,1)S(1)}, bf16[2,256,256]{2,1,0:T(8,128)(2,1)}, u32[]{:S(2)}) copy-start(bf16[2,256,256]{2,1,0:T(8,128)(2,1)} %get-tuple-element.5.down_ref.up_ref) | copy-start | bytes 786436
  134.9 8.5 %copy-start.6 = (bf16[2,256,256]{2,1,0:T(8,128)(2,1)S(1)}, bf16[2,256,256]{2,1,0:T(8,128)(2,1)}, u32[]{:S(2)}) copy-start(bf16[2,256,256]{2,1,0:T(8,128)(2,1)} %get-tuple-element.6.up_ref.down_ref) | copy-start | bytes 786436
  141.8 57.1 %collective-permute-start.6 = (bf16[1,48,8,128]{3,2,1,0:T(8,128)(2,1)S(1)}, bf16[1,48,8,128]{3,2,1,0:T(8,128)(2,1)S(1)}, u32[]{:S(2)}, u32[]{:S(2)}) collective-permute-start(bf16[1,48,8,128]{3,2,1,0:T(8,128)(2,1)S(1)} %get-tuple-element.20), channel_id=1, source_target_pairs={{0,1},{1,2},{2,3},{3,0},{4,5},{5,6},{6,7},{7,4},{8,9},{9,10},{10,1... | collective-permute-start | bytes 294920 | tf_op jit(solution)/shard_map/ppermute | solution.py:26
  143.3 55.6 %collective-permute-start.7 = (bf16[1,48,8,128]{3,2,1,0:T(8,128)(2,1)S(1)}, bf16[1,48,8,128]{3,2,1,0:T(8,128)(2,1)S(1)}, u32[]{:S(2)}, u32[]{:S(2)}) collective-permute-start(bf16[1,48,8,128]{3,2,1,0:T(8,128)(2,1)S(1)} %get-tuple-element.21), channel_id=1, source_target_pairs={{1,0},{2,1},{3,2},{0,3},{5,4},{6,5},{7,6},{4,7},{9,8},{10,9},{11,1... | collective-permute-start | bytes 294920 | tf_op jit(solution)/shard_map/ppermute | solution.py:28
  198.9 2.0 copy-start.9
  201.0 1.7 copy-start.10
  202.6 1.7 copy-start.11
  207.2 3.4 %copy-start.14 = (bf16[1,32,64,128]{3,2,1,0:T(8,128)(2,1)S(1)}, bf16[1,32,64,128]{3,2,1,0:T(8,128)(2,1)}, u32[]{:S(2)}) copy-start(bf16[1,32,64,128]{3,2,1,0:T(8,128)(2,1)} %param.9) | copy-start | bytes 1572868

commit v2 on v1

v2 whole, which is shorter than its diff:
```python
import functools
import math

import jax
import jax.numpy as jnp
from jax import lax
from jax.experimental import pallas as pl
from jax.experimental.pallas import tpu as pltpu
from jax.sharding import PartitionSpec as P

MDEV = 16
HW = 8


TANH_SCALE = 0.7978845608028654
CUBIC_TERM = 0.044715


def gelu_parts(values):
    tanh_input = TANH_SCALE * (values + CUBIC_TERM * values * values * values)
    hyper = jnp.tanh(tanh_input)
    result = 0.5 * values * (1.0 + hyper)
    derivative = 0.5 * (1.0 + hyper) + 0.5 * values * (1.0 - hyper * hyper) * TANH_SCALE * (
        1.0 + 3.0 * CUBIC_TERM * values * values
    )
    return (result, derivative)


def mode_tables(lon_count, mode_count):
    angles_int = (
        jnp.arange(lon_count, dtype=jnp.int32)[:, None]
        * jnp.arange(mode_count, dtype=jnp.int32)[None, :]
        % lon_count
    )
    angles = angles_int.astype(jnp.float32) * (2.0 * math.pi / lon_count)
    stacked = jnp.stack([jnp.cos(angles), -jnp.sin(angles)], axis=1)
    orders = jnp.arange(mode_count, dtype=jnp.int32)
    factor = jnp.where(orders == 0, 1.0, 2.0).astype(jnp.float32)
    to_modes = (stacked * (2.0 * math.pi / lon_count)).astype(jnp.bfloat16)
    from_modes = (stacked * factor[None, None, :]).astype(jnp.bfloat16)
    return (to_modes, from_modes)


STEP = 16


def legendre_kernel(gain_ref, back_ref, orders_ref, trig_ref, weighted_ref, plain_ref):
    order_share, degree_count, _ = plain_ref.shape
    cosine = trig_ref[0:1, :]
    quadrature = trig_ref[1:2, :]

    def block(index, state):
        carried = []
        for e in range(order_share):
            value, previous, log_scale = state[3 * e : 3 * e + 3]
            order = orders_ref[e]
            rows = []
            for step in range(STEP):
                degree = index * STEP + step
                active = degree > order
                following = gain_ref[e, degree] * (cosine * value) - back_ref[e, degree] * previous
                previous = jnp.where(active, value, previous)
                value = jnp.where(active, following, value)
                rows.append(jnp.where(degree >= order, value, 0.0))
            stacked = jnp.concatenate(rows, axis=0) * jnp.exp(log_scale)
            place = pl.ds(pl.multiple_of(index * STEP, STEP), STEP)
            plain_ref[e, place, :] = stacked.astype(jnp.bfloat16)
            weighted_ref[e, place, :] = (stacked * quadrature).astype(jnp.bfloat16)
            largest = jnp.maximum(jnp.abs(value), jnp.abs(previous))
            carried += [value / largest, previous / largest, log_scale + jnp.log(largest)]
        return tuple(carried)

    start = []
    for e in range(order_share):
        seed = trig_ref[2 + e : 3 + e, :]
        start += [jnp.ones_like(seed), jnp.zeros_like(seed), seed]
    lax.fori_loop(0, degree_count // STEP, block, tuple(start))


def legendre_tables(orders, degree_count, lat_count):
    order_share = orders.shape[0]
    colatitude = math.pi * (jnp.arange(lat_count, dtype=jnp.float32) + 0.5) / lat_count
    sine_part = jnp.sin(colatitude)
    order_real = orders.astype(jnp.float32)
    seed_log = 0.5 * (
        jnp.log((2.0 * order_real + 1.0) / (4.0 * math.pi))
        + lax.lgamma(order_real + 0.5)
        - lax.lgamma(order_real + 1.0)
        - 0.5 * math.log(math.pi)
    )
    seed_log = seed_log[:, None] + order_real[:, None] * jnp.log(sine_part)[None, :]
    degree_real = jnp.arange(degree_count, dtype=jnp.float32)[None, :]
    order_row = order_real[:, None]
    forward_gain = jnp.sqrt(
        jnp.maximum(4.0 * degree_real * degree_real - 1.0, 1.0)
        / jnp.maximum(degree_real * degree_real - order_row * order_row, 1.0)
    )
    backward_gain = jnp.sqrt(
        jnp.maximum((degree_real - 1.0) ** 2 - order_row * order_row, 0.0)
        / jnp.maximum(4.0 * (degree_real - 1.0) ** 2 - 1.0, 1.0)
    )
    trig = jnp.concatenate(
        [
            jnp.cos(colatitude)[None, :],
            (math.pi / lat_count * sine_part)[None, :],
            seed_log,
        ],
        axis=0,
    )
    table = jax.ShapeDtypeStruct((order_share, degree_count, lat_count), jnp.bfloat16)
    smem = pl.BlockSpec(memory_space=pltpu.SMEM)
    vmem = pl.BlockSpec(memory_space=pltpu.VMEM)
    return pl.pallas_call(
        legendre_kernel,
        out_shape=(table, table),
        in_specs=[smem, smem, smem, vmem],
        out_specs=(vmem, vmem),
        name="legendre_tables",
    )(forward_gain, forward_gain * backward_gain, orders, trig)


CHUNKS = 2
EDGE = 2 * HW


def spectral_kernel(
    lat_count,
    lon_count,
    adjoint,
    data_ref,
    first_ref,
    down_ref,
    up_ref,
    last_ref,
    mix_ref,
    out_ref,
    padded_ref,
    part_out,
    pair_in,
    pair_out,
    cross_in,
    rows_out,
    rows_in,
    deg_out,
    deg_in,
    mixed_out,
    mixed_in,
    zonal_out,
    zonal_in,
    grid_out,
    grid_in,
    blended,
    pair_sems,
    cross_sems,
    lat_sems,
    gather_sems,
    relay_sems,
    halo_sems,
):
    row_count, lon_dev, channels = data_ref.shape
    order_share = down_ref.shape[0]
    degree_dev = mix_ref.shape[0]
    wide = 2 * channels
    share = lat_count * order_share
    modes = 2 * share
    chips = lon_count // 2
    rows_each = row_count // CHUNKS
    degrees_each = degree_dev // CHUNKS
    lat_me = lax.axis_index("lat")
    lon_me = lax.axis_index("lon")
    chip = lon_me // 2
    core = lax.rem(lon_me, 2)
    mate = 2 * chip + 1 - core
    lat_peers = [lax.rem(lat_me + step, lat_count) for step in range(1, lat_count)]
    chip_peers = [lax.rem(chip + step, chips) for step in range(1, chips)]
    lat_next = lax.rem(lat_me + 1, lat_count)
    lat_last = lax.rem(lat_me + lat_count - 1, lat_count)
    lon_next = lax.rem(lon_me + 1, lon_count)
    lon_last = lax.rem(lon_me + lon_count - 1, lon_count)
    halo_rows = {
        0: (lat_me, slice(0, row_count), slice(HW, HW + row_count)),
        1: (lat_next, slice(row_count - HW, row_count), slice(0, HW)),
        2: (lat_last, slice(0, HW), slice(HW + row_count, 2 * HW + row_count)),
    }
    halo_columns = {
        0: (lon_me, slice(0, lon_dev), slice(EDGE, EDGE + lon_dev)),
        1: (lon_next, slice(lon_dev - EDGE, lon_dev), slice(0, EDGE)),
        2: (lon_last, slice(0, EDGE), slice(EDGE + lon_dev, 2 * EDGE + lon_dev)),
    }

    barrier = pltpu.get_barrier_semaphore()

    def greet(lat, lon):
        pl.semaphore_signal(
            barrier, inc=1, device_id=(lat, lon), device_id_type=pl.DeviceIdType.MESH
        )

    for peer in lat_peers:
        greet(peer, lon_me)
    for step in range(1, lon_count):
        greet(lat_me, lax.rem(lon_me + step, lon_count))
    for lat in (lat_next, lat_last):
        for lon in (lon_next, lon_last):
            greet(lat, lon)
    greetings = lat_count - 1 + lon_count - 1 + 4

    started = []

    def copying(source, target, sems, place, came, device):
        return pltpu.make_async_remote_copy(
            src_ref=source,
            dst_ref=target,
            send_sem=sems.at[(0,) + place],
            recv_sem=sems.at[(1,) + came],
            device_id=device,
            device_id_type=pl.DeviceIdType.MESH,
        )

    def push(source, target, sems, place, came, device):
        copy = copying(source, target, sems, place, came, device)
        copy.start()
        started.append(copy)

    def arrived(target, sems, came):
        copying(target, target, sems, came, came, (lat_me, mate)).wait_recv()

    def rows_of(number):
        return pl.ds(number * rows_each, rows_each)

    def transform(number):
        group = 8

        def body(index, carry):
            for step in range(group):
                row = number * rows_each + index * group + step
                part = jnp.dot(
                    first_ref[...], data_ref[row], preferred_element_type=jnp.float32
                ).astype(jnp.bfloat16)
                for other in range(chips):
                    for side in range(2):
                        begin = (2 * other + side) * modes
                        part_out[side, other, row] = part[begin : begin + modes]
            return carry

        lax.fori_loop(0, rows_each // group, body, 0)

    def lat_push(number, piece, source, target):
        for peer in lat_peers:
            push(
                source(peer),
                target(lat_me),
                lat_sems,
                (number, piece, peer),
                (number, piece, lat_me),
                (peer, lon_me),
            )

    def lat_arrived(number, piece, target):
        for peer in lat_peers:
            arrived(target(peer), lat_sems, (number, piece, peer))

    for number in range(CHUNKS):
        transform(number)
        if number == 0:
            pl.semaphore_wait(barrier, greetings)
        push(
            part_out.at[1 - core, :, rows_of(number)],
            pair_in.at[:, rows_of(number)],
            pair_sems,
            (number,),
            (number,),
            (lat_me, mate),
        )
    for r, (lat, from_rows, to_rows) in halo_rows.items():
        for c, (lon, from_columns, to_columns) in halo_columns.items():
            if r or c:
                push(
                    data_ref.at[from_rows, from_columns],
                    padded_ref.at[to_rows, to_columns],
                    halo_sems,
                    (3 * r + c,),
                    (3 * r + c,),
                    (lat, lon),
                )
    for number in range(CHUNKS):
        piece = rows_of(number)
        arrived(pair_in.at[:, piece], pair_sems, (number,))
        for other in chip_peers:
            pair_out[other, piece] = (
                part_out[core, other, piece].astype(jnp.float32)
                + pair_in[other, piece].astype(jnp.float32)
            ).astype(jnp.bfloat16)
            push(
                pair_out.at[other, piece],
                cross_in.at[chip, piece],
                cross_sems,
                (number, other),
                (number, chip),
                (lat_me, 2 * other + core),
            )
    padded_ref[HW : HW + row_count, EDGE : EDGE + lon_dev] = data_ref[...]
    for number in range(CHUNKS):
        piece = rows_of(number)
        total = part_out[core, chip, piece].astype(jnp.float32) + pair_in[chip, piece].astype(
            jnp.float32
        )
        for other in chip_peers:
            arrived(cross_in.at[other, piece], cross_sems, (number, other))
            total = total + cross_in[other, piece].astype(jnp.float32)
        begin = number * rows_each
        rows_out[:, :, :, begin : begin + rows_each] = (
            jnp.swapaxes(total, 0, 1)
            .astype(jnp.bfloat16)
            .reshape(lat_count, order_share, 2, rows_each, channels)
        )
        lat_push(
            0,
            number,
            lambda peer: rows_out.at[peer, :, :, piece],
            lambda peer: rows_in.at[peer, :, :, piece],
        )
    rows_in[lat_me] = rows_out[lat_me]
    for number in range(CHUNKS):
        piece = rows_of(number)
        lat_arrived(0, number, lambda peer: rows_in.at[peer, :, :, piece])

    for e in range(order_share):
        columns = jnp.concatenate(
            [rows_in[:, e, part].reshape(lat_count * row_count, channels) for part in range(2)],
            axis=1,
        )
        degrees = jnp.dot(down_ref[e], columns, preferred_element_type=jnp.float32)
        deg_out[:, e] = degrees.astype(jnp.bfloat16).reshape(lat_count, degree_dev, wide)
    for number in range(CHUNKS):
        piece = pl.ds(number * degrees_each, degrees_each)
        lat_push(
            1,
            number,
            lambda peer: deg_out.at[peer, :, piece],
            lambda peer: deg_in.at[peer, :, piece],
        )
    deg_in[lat_me] = deg_out[lat_me]

    for number in range(CHUNKS):
        begin = number * degrees_each
        piece = pl.ds(begin, degrees_each)
        lat_arrived(1, number, lambda peer: deg_in.at[peer, :, piece])
        by_degree = deg_in[:, :, begin : begin + degrees_each].reshape(share, degrees_each, wide)
        turned = jnp.swapaxes(by_degree.astype(jnp.float32), 0, 1).astype(jnp.bfloat16)
        for step in range(degrees_each):
            degree = begin + step
            pair = jnp.concatenate([turned[step, :, :channels], turned[step, :, channels:]], axis=0)
            if adjoint:
                weights = jnp.concatenate([mix_ref[degree, 0], mix_ref[degree, 1]], axis=0)
                product = lax.dot_general(
                    pair, weights, (((1,), (1,)), ((), ())), preferred_element_type=jnp.float32
                )
            else:
                weights = jnp.concatenate([mix_ref[degree, 0], mix_ref[degree, 1]], axis=1)
                product = jnp.dot(pair, weights, preferred_element_type=jnp.float32)
            sign = -1.0 if adjoint else 1.0
            blended[step, :, :channels] = (
                product[:share, :channels] - sign * product[share:, channels:]
            )
            blended[step, :, channels:] = (
                sign * product[:share, channels:] + product[share:, :channels]
            )
        mixed_out[:, :, begin : begin + degrees_each] = (
            jnp.swapaxes(blended[...], 0, 1)
            .astype(jnp.bfloat16)
            .reshape(lat_count, order_share, degrees_each, wide)
        )
        lat_push(
            2,
            number,
            lambda peer: mixed_out.at[peer, :, piece],
            lambda peer: mixed_in.at[peer, :, piece],
        )
    mixed_in[lat_me] = mixed_out[lat_me]
    for number in range(CHUNKS):
        piece = pl.ds(number * degrees_each, degrees_each)
        lat_arrived(2, number, lambda peer: mixed_in.at[peer, :, piece])

    for e in range(order_share):
        spectrum = mixed_in[:, e].reshape(lat_count * degree_dev, wide)
        zonal = lax.dot_general(
            up_ref[e], spectrum, (((0,), (0,)), ((), ())), preferred_element_type=jnp.float32
        ).astype(jnp.bfloat16)
        for part in range(2):
            zonal_out[:, e, part] = zonal[:, part * channels : (part + 1) * channels].reshape(
                lat_count, row_count, channels
            )
    for number in range(CHUNKS):
        piece = rows_of(number)
        lat_push(
            3,
            number,
            lambda peer: zonal_out.at[peer, :, :, piece],
            lambda peer: zonal_in.at[peer, :, :, piece],
        )
    zonal_in[lat_me] = zonal_out[lat_me]

    for number in range(CHUNKS):
        piece = rows_of(number)
        begin = number * rows_each
        lat_arrived(3, number, lambda peer: zonal_in.at[peer, :, :, piece])
        by_order = zonal_in[:, :, :, begin : begin + rows_each].reshape(modes, rows_each, channels)
        grid_out[piece] = jnp.swapaxes(by_order.astype(jnp.float32), 0, 1).astype(jnp.bfloat16)
        for lon in [2 * other + core for other in chip_peers] + [mate]:
            push(
                grid_out.at[piece],
                grid_in.at[lon_me, piece],
                gather_sems,
                (number, lon),
                (number, lon_me),
                (lat_me, lon),
            )
        grid_in[lon_me, piece] = grid_out[piece]
    for number in range(CHUNKS):
        piece = rows_of(number)
        for other in chip_peers:
            slot = 2 * other + core
            arrived(grid_in.at[slot, piece], gather_sems, (number, slot))
            push(
                grid_in.at[slot, piece],
                grid_in.at[slot, piece],
                relay_sems,
                (number, slot),
                (number, slot),
                (lat_me, mate),
            )
    for number in range(CHUNKS):
        piece = rows_of(number)
        arrived(grid_in.at[mate, piece], gather_sems, (number, mate))
        for other in chip_peers:
            slot = 2 * other + 1 - core
            arrived(grid_in.at[slot, piece], relay_sems, (number, slot))

        def restore(index, carry):
            for step in range(8):
                row = number * rows_each + index * 8 + step
                every = grid_in[:, row].reshape(lon_count * modes, channels)
                out_ref[row] = jnp.dot(
                    last_ref[...], every, preferred_element_type=jnp.float32
                ).astype(jnp.bfloat16)
            return carry

        lax.fori_loop(0, rows_each // 8, restore, 0)

    for r, (lat, from_rows, to_rows) in halo_rows.items():
        for c, (lon, from_columns, to_columns) in halo_columns.items():
            if r or c:
                arrived(padded_ref.at[to_rows, to_columns], halo_sems, (3 * r + c,))
    for copy in started:
        copy.wait_send()


def spectral_pass(lat_count, lon_count, adjoint, data, first, down, up, last, mix):
    row_count, lon_dev, channels = data.shape
    order_share = down.shape[0]
    degree_dev = mix.shape[0]
    share = lat_count * order_share
    wide = 2 * channels
    chips = lon_count // 2
    bf16 = jnp.bfloat16
    part = pltpu.VMEM((chips, row_count, 2 * share, channels), bf16)
    rows = pltpu.VMEM((lat_count, order_share, 2, row_count, channels), bf16)
    degrees = pltpu.VMEM((lat_count, order_share, degree_dev, wide), bf16)
    vmem = pl.BlockSpec(memory_space=pltpu.VMEM)
    return pl.pallas_call(
        functools.partial(spectral_kernel, lat_count, lon_count, adjoint),
        out_shape=(
            jax.ShapeDtypeStruct(data.shape, bf16),
            jax.ShapeDtypeStruct((row_count + 2 * HW, lon_dev + 2 * EDGE, channels), bf16),
        ),
        in_specs=[vmem] * 6,
        out_specs=(vmem, vmem),
        scratch_shapes=[
            pltpu.VMEM((2, chips, row_count, 2 * share, channels), bf16),
            part,
            part,
            part,
            rows,
            rows,
            degrees,
            degrees,
            degrees,
            degrees,
            rows,
            rows,
            pltpu.VMEM((row_count, 2 * share, channels), bf16),
            pltpu.VMEM((lon_count, row_count, 2 * share, channels), bf16),
            pltpu.VMEM((degree_dev // CHUNKS, share, wide), jnp.float32),
            pltpu.SemaphoreType.DMA((2, CHUNKS)),
            pltpu.SemaphoreType.DMA((2, CHUNKS, chips)),
            pltpu.SemaphoreType.DMA((2, 4, CHUNKS, lat_count)),
            pltpu.SemaphoreType.DMA((2, CHUNKS, lon_count)),
            pltpu.SemaphoreType.DMA((2, CHUNKS, lon_count)),
            pltpu.SemaphoreType.DMA((2, 9)),
        ],
        compiler_params=pltpu.CompilerParams(
            collective_id=1 if adjoint else 0,
            has_side_effects=True,
            vmem_limit_bytes=48 * 1024 * 1024,
        ),
        name="spectral_adjoint" if adjoint else "spectral_forward",
    )(data, first, down, up, last, mix)


def toeplitz(taps, count):
    spread = [
        pltpu.roll(
            jnp.broadcast_to(taps[k : k + 1, :], (count, taps.shape[1])),
            0,
            1,
            stride=1,
            stride_axis=0,
        )
        for k in range(taps.shape[0])
    ]
    return jnp.concatenate(spread, axis=0).astype(jnp.bfloat16)


def stretch(padded_ref, whole_ref):
    width = whole_ref.shape[1]

    def body(row, carry):
        whole_ref[row] = padded_ref[row].astype(jnp.float32)[HW : HW + width]
        return carry

    lax.fori_loop(0, whole_ref.shape[0], body, 0)


def local_kernel(
    rows_ref, taps_ref, padded_ref, spectral_ref, cotangent_ref, weight_ref, out_ref, mix_ref, whole
):
    row_count, lon_dev, channels = out_ref.shape
    width = whole.shape[1]
    kernel_count = taps_ref.shape[1]
    band_count = rows_ref.shape[1]
    stretch(padded_ref, whole)
    spare = jnp.zeros((taps_ref.shape[2] - band_count * width, channels), jnp.float32)

    def one(row):
        sources = jnp.concatenate(
            [whole[rows_ref[row, band]] for band in range(band_count)] + [spare], axis=0
        ).astype(jnp.bfloat16)
        terms = jnp.dot(
            toeplitz(taps_ref[row], lon_dev), sources, preferred_element_type=jnp.float32
        ).astype(jnp.bfloat16)
        flat = jnp.concatenate(
            [terms[k * lon_dev : (k + 1) * lon_dev] for k in range(kernel_count)], axis=1
        )
        pre_act = spectral_ref[row].astype(jnp.float32) + jnp.dot(
            flat, weight_ref[...], preferred_element_type=jnp.float32
        )
        activation, derivative = gelu_parts(pre_act)
        field = whole[row + HW][HW : HW + lon_dev]
        out_ref[row] = (field + activation).astype(jnp.bfloat16)
        mix_ref[row] = (cotangent_ref[row].astype(jnp.float32) * derivative).astype(jnp.bfloat16)

    def body(index, carry):
        for step in range(4):
            one(4 * index + step)
        return carry

    lax.fori_loop(0, row_count // 4, body, 0)


def local_adjoint_kernel(
    rows_ref, taps_ref, padded_ref, spectral_ref, cotangent_ref, weight_ref, out_ref, whole, total
):
    row_count, lon_dev, channels = out_ref.shape
    tall, width, _ = whole.shape
    band_count = rows_ref.shape[1]
    kernel_count = weight_ref.shape[1] // channels
    stretch(padded_ref, whole)
    spare = jnp.zeros((taps_ref.shape[2] - kernel_count * width, channels), jnp.bfloat16)
    total[...] = jnp.zeros_like(total)

    def body(index, carry):
        pieces = []
        for step in range(4):
            row = 4 * index + step
            grads = jnp.dot(
                whole[row].astype(jnp.bfloat16), weight_ref[...], preferred_element_type=jnp.float32
            ).astype(jnp.bfloat16)
            stacked = jnp.concatenate(
                [grads[:, k * channels : (k + 1) * channels] for k in range(kernel_count)] + [spare],
                axis=0,
            )
            pieces.append(
                jnp.dot(
                    toeplitz(taps_ref[row], lon_dev), stacked, preferred_element_type=jnp.float32
                )
            )
        for step in range(4):
            for band in range(band_count):
                target = rows_ref[4 * index + step, band]
                total[target] += pieces[step][band * lon_dev : (band + 1) * lon_dev]
        return carry

    lax.fori_loop(0, tall // 4, body, 0)
    out_ref[...] = (
        cotangent_ref[...].astype(jnp.float32)
        + spectral_ref[...].astype(jnp.float32)
        + total[2 * HW : 2 * HW + row_count]
    ).astype(jnp.bfloat16)


def tap_rows(basis, width):
    flat = jnp.pad(basis, ((0, 0), (0, 0), (0, 0), (0, width - basis.shape[3])))
    flat = flat.reshape(basis.shape[0], basis.shape[1], basis.shape[2] * width)
    lanes = -(-flat.shape[2] // 128) * 128
    return jnp.pad(flat, ((0, 0), (0, 0), (0, lanes - flat.shape[2]))).astype(jnp.float32)


def per_device(fields, cotangent, spectral_weight, local_weight, filter_basis, neighbor_rows):
    lat_count = lax.axis_size("lat")
    lon_count = lax.axis_size("lon")
    lat_index = lax.axis_index("lat")
    lon_index = lax.axis_index("lon")
    _, lat_dev, lon_dev, channels = fields.shape
    degree_dev = spectral_weight.shape[0]
    kernel_count = filter_basis.shape[0]
    total_lat = lat_dev * lat_count
    total_lon = lon_dev * lon_count
    order_share = MDEV // lat_count
    width = lon_dev + 2 * HW
    tall = lat_dev + 2 * HW
    to_modes, from_modes = mode_tables(total_lon, MDEV * lon_count)
    table_shape = (lon_dev, 2, lon_count, lat_count, order_share)
    to_modes = lax.dynamic_slice_in_dim(to_modes, lon_index * lon_dev, lon_dev, 0)
    from_modes = lax.dynamic_slice_in_dim(from_modes, lon_index * lon_dev, lon_dev, 0)
    to_modes = to_modes.reshape(table_shape).transpose(0, 2, 3, 4, 1).reshape(lon_dev, -1)
    from_modes = from_modes.reshape(table_shape).transpose(0, 2, 3, 4, 1).reshape(lon_dev, -1)
    orders = (
        lon_index * MDEV + lat_index * order_share + jnp.arange(order_share, dtype=jnp.int32)
    )
    weighted, unweighted = legendre_tables(orders, degree_dev * lat_count, total_lat)
    row_base = lat_index * lat_dev
    near_rows = lax.dynamic_slice_in_dim(
        jnp.pad(neighbor_rows, ((HW, HW), (0, 0))), row_base, tall, 0
    )
    near_basis = lax.dynamic_slice_in_dim(
        jnp.pad(filter_basis, ((0, 0), (HW, HW), (0, 0), (0, 0))), row_base, tall, 1
    )
    sources = near_rows[HW : HW + lat_dev] - row_base + HW
    targets = jnp.clip(near_rows - row_base + 2 * HW, 0, lat_dev + 4 * HW - 1)
    taps = tap_rows(near_basis[:, HW : HW + lat_dev].transpose(1, 0, 2, 3), width)
    back_taps = tap_rows(near_basis[..., ::-1].transpose(1, 2, 0, 3), width)
    smem = pl.BlockSpec(memory_space=pltpu.SMEM)
    vmem = pl.BlockSpec(memory_space=pltpu.VMEM)
    grid = jax.ShapeDtypeStruct((lat_dev, lon_dev, channels), jnp.bfloat16)
    whole = pltpu.VMEM((tall, width, channels), jnp.float32)
    params = pltpu.CompilerParams(vmem_limit_bytes=40 * 1024 * 1024)

    spectral, padded = spectral_pass(
        lat_count,
        lon_count,
        False,
        fields[0],
        to_modes.T,
        weighted,
        unweighted,
        from_modes,
        spectral_weight,
    )
    block_output, grad_mix = pl.pallas_call(
        local_kernel,
        out_shape=(grid, grid),
        in_specs=[smem] + [vmem] * 5,
        out_specs=(vmem, vmem),
        scratch_shapes=[whole],
        compiler_params=params,
        name="local_forward",
    )(sources, taps, padded, spectral, cotangent[0], local_weight.reshape(-1, channels))
    grad_spectral, grad_padded = spectral_pass(
        lat_count,
        lon_count,
        True,
        grad_mix,
        from_modes.T,
        unweighted,
        weighted,
        to_modes,
        spectral_weight,
    )
    input_grad = pl.pallas_call(
        local_adjoint_kernel,
        out_shape=grid,
        in_specs=[smem] + [vmem] * 5,
        out_specs=vmem,
        scratch_shapes=[whole, pltpu.VMEM((lat_dev + 4 * HW, lon_dev, channels), jnp.float32)],
        compiler_params=params,
        name="local_adjoint",
    )(
        targets,
        back_taps,
        grad_padded,
        grad_spectral,
        cotangent[0],
        local_weight.transpose(2, 0, 1).reshape(channels, kernel_count * channels),
    )
    return (block_output[None], input_grad[None])


def solution(mesh):
    in_specs = (
        P(None, "lat", "lon", None),
        P(None, "lat", "lon", None),
        P("lat", None, None, None),
        P(),
        P(),
        P(),
    )
    out_specs = (P(None, "lat", "lon", None), P(None, "lat", "lon", None))
    return jax.shard_map(
        per_device, mesh=mesh, in_specs=in_specs, out_specs=out_specs, check_vma=False
    )
```

time: 216 us -> 139 us (0.64); the launches traced: 213 us -> 139 us
  matrix products: 36.3 us -> 0 us
  other arithmetic: 14.6 us -> 2.61 us
  starting transfers between devices: 11.4 us -> 0 us
  local copies, waits for them, and re-layouts: 25.9 us -> 15.7 us
  waiting for transfers between devices: 7.85 us -> 0 us
  Pallas kernels: 116 us -> 119 us
    dot_general x16 -> x0, matrix products: 36.3 us -> none  [the longest x2 6.88 us: per_device(): jnp.einsum('kift,aitc->kaifc', banded, sources, preferred_element_type=jn...]
    ppermute x8 -> x0, starting transfers between devices: 11.4 us -> none  [the longest x4 5.89 us: extended(): lax.ppermute(tail, axis, [(i, (i + 1) % count) for i in range(count)])]
    ppermute x8 -> x0, waiting for transfers between devices: 7.85 us -> none  [the longest x4 5.23 us: extended(): lax.ppermute(head, axis, [((i + 1) % count, i) for i in range(count)])]
    gather x5 -> x0, local copies, waits for them, and re-layouts: 6.9 us -> none  [the longest x3 4.43 us: per_device(): sources = jnp.take(padded, source_rows, axis=1)]
    slice x9 -> x0, local copies, waits for them, and re-layouts: 5.55 us -> none  [the longest x1 1.72 us: extended(): head = lax.slice_in_dim(cells, 0, width, axis=dim)]
    pallas_call x2 -> x4, Pallas kernels: 112 us -> 116 us  [the longest x2 97.4 us: spectral_pass(): pl.pallas_call(functools.partial(spectral_kernel, lat_count, lon_count, a...]
    unnamed x64 -> x46, local copies, waits for them, and re-layouts: 11.5 us -> 14.6 us
    another operation x3 -> x0, other arithmetic: 3.02 us -> none  [the longest x2 2.93 us: per_device(): jnp.stack([spectral_weight[:, 0].transpose(0, 2, 1), -spectral_weight[:,...]
  transfers between devices with their start and end apart: 8 -> 0, of which waited for: 4 -> 0; matrix products, arithmetic and copies ran while one was open for 18% -> 0% of each run, Pallas kernels for 54% -> 0%
where the time goes in v2:
time: 139 us
  Pallas kernels  119 us (86%)
  local copies, waits for them, and re-layouts  15.7 us (11%)
  other arithmetic  2.61 us (2%)
    pallas_call x2, Pallas kernels, spectral_pass(): pl.pallas_call(functools.partial(spectral_kernel, lat_count, lon_count, a...  97.4 us
    unnamed x46, local copies, waits for them, and re-layouts  14.6 us
    pallas_call x1, Pallas kernels, per_device(): pl.pallas_call(local_adjoint_kernel, out_shape=grid, in_specs=[smem] + [v...  9.91 us
    pallas_call x1, Pallas kernels, per_device(): pl.pallas_call(local_kernel, out_shape=(grid, grid), in_specs=[smem] + [v...  8.42 us
    pallas_call x1, Pallas kernels, legendre_tables(): pl.pallas_call(legendre_kernel, out_shape=(table, table), in_specs=[smem,...  3.62 us

profile of v2, /device:TPU:1, one launch (start us, length us, event | category | flops | bytes accessed | tf_op | source)
XLA Modules:
  0.0 138.5 jit_solution(10892145423940393293)
XLA Ops:
  0.6 0.1 add_multiply_fusion.2
  0.7 0.5 iota_add_fusion
  1.3 0.1 multiply_add_fusion
  1.4 0.1 sine_multiply_fusion
  1.5 0.6 pad_maximum_fusion.trig_ref
  2.1 0.7 sqrt_multiply_fusion
  2.7 3.6 %legendre_tables.1 = (bf16[2,256,256]{2,1,0:T(8,128)(2,1)}, bf16[2,256,256]{2,1,0:T(8,128)(2,1)}) custom-call(f32[2,256]{1,0:T(2,128)} %get-tuple-element.21.gain_ref, f32[2,256]{1,0:T(2,128)} %get-tuple-element.20.back_ref, s32[2]{0:T(128)} %get-tuple-element.26.orders_ref, f32[4,256]{1,0:T(4,128)} %pad_maximum_fusion.trig_ref), custom_call_target="tpu_custom_call" | custom-call | tf_op jit(solution)/shard_map/legendre_tables/pallas_call | solution.py:113
  6.4 0.3 sine_negate_fusion
  6.7 0.1 multiply_convert_fusion
  6.8 0.1 copy.37.last_ref
  7.0 0.0 copy-start
  7.0 1.6 %copy-done = bf16[32,2,128,128]{3,2,1,0:T(8,128)(2,1)S(1)} copy-done((bf16[32,2,128,128]{3,2,1,0:T(8,128)(2,1)S(1)}, bf16[32,2,128,128]{3,2,1,0:T(8,128)(2,1)}, u32[]{:S(2)}) %copy-start) | copy-done | bytes 2097176
  8.6 0.0 copy-start.7
  8.6 0.9 copy-done.7
  9.5 0.9 copy-done.9
  10.5 0.0 copy-start.11
  10.5 1.0 copy-done.11
  11.5 0.0 copy-start.21
  11.5 0.0 copy-start.19
  11.5 49.7 %spectral_forward.1 = (bf16[32,64,128]{2,1,0:T(8,128)(2,1)S(1)}, bf16[48,96,128]{2,1,0:T(8,128)(2,1)S(1)}) custom-call(bf16[32,64,128]{2,1,0:T(8,128)(2,1)S(1)} %bitcast.27, bf16[128,64]{1,0:T(8,128)(2,1)S(1)} %bitcast.32, bf16[2,256,256]{2,1,0:T(8,128)(2,1)S(1)} %copy-done.7, bf16[2,256,256]{2,1,0:T(8,128)(2,1)S(1)} %copy-done.9, ...), custom_call_target="tpu_custom_call" | custom-call | tf_op jit(solution)/shard_map/spectral_forward/pallas_call | solution.py:470
  61.2 0.0 copy-start.5
  61.2 1.0 copy-done.5
  62.3 0.0 copy-start.12
  62.3 0.8 copy-done.12
  63.1 0.0 copy-start.2
  63.1 0.0 copy-start.18
  63.1 0.0 copy-done.21
  63.1 0.1 copy.32
  63.2 0.0 copy-done.19
  63.2 0.1 fusion.7
  63.4 0.2 copy.54
  63.6 0.1 pad.26.clone
  63.6 0.0 copy-start.10
  63.6 0.1 reshape.298
  63.8 0.3 copy-done.2
  64.1 0.0 copy-done.18
  64.1 0.0 copy-start.6
  64.1 1.3 copy-done.6
  65.4 0.0 copy-start.13
  65.4 1.0 copy-done.13
  66.4 0.0 copy-start.1
  66.4 8.4 %local_forward.1 = (bf16[32,64,128]{2,1,0:T(8,128)(2,1)}, bf16[32,64,128]{2,1,0:T(8,128)(2,1)S(1)}) custom-call(s32[32,3]{1,0:T(8,128)S(1)} %fusion.13.rows_ref, f32[32,3,256]{2,1,0:T(4,128)S(1)} %pad_convert_fusion.1.taps_ref, bf16[48,96,128]{2,1,0:T(8,128)(2,1)S(1)} %copy-done.6, bf16[32,64,128]{2,1,0:T(8,128)(2,1)S(1)} %copy-done.13, ...), custom_call_target="tpu_custom_call" | custom-call | tf_op jit(solution)/shard_map/local_forward/pallas_call | solution.py:669
  74.9 0.0 copy-start.14
  74.9 0.8 copy-done.14
  75.6 0.1 copy.41.last_ref
  75.7 0.0 copy-done.10
  75.7 0.0 copy-done.1
  75.8 0.0 copy-done.8
  75.8 0.0 copy-start.15
  75.8 1.0 copy-done.15
  76.8 0.0 copy-start.20
  76.8 47.6 %spectral_adjoint.1 = (bf16[32,64,128]{2,1,0:T(8,128)(2,1)S(1)}, bf16[48,96,128]{2,1,0:T(8,128)(2,1)S(1)}) custom-call(bf16[32,64,128]{2,1,0:T(8,128)(2,1)S(1)} %copy-done.15, bf16[128,64]{1,0:T(8,128)(2,1)S(1)} %bitcast.31, bf16[2,256,256]{2,1,0:T(8,128)(2,1)S(1)} %copy-done.10, bf16[2,256,256]{2,1,0:T(8,128)(2,1)S(1)} %copy-done.8, ...), custom_call_target="tpu_custom_call" | custom-call | tf_op jit(solution)/shard_map/spectral_adjoint/pallas_call | solution.py:470
  124.5 0.0 copy-start.3
  124.5 1.0 copy-done.3
  125.5 0.8 copy-done.16
  126.3 0.0 copy-done.20
  126.3 0.1 pad_dynamic-slice_fusion.1
  126.5 0.1 pad.28
  126.6 0.2 copy.40
  126.8 0.1 pad_convert_fusion.taps_ref
  126.8 0.1 copy.42.weight_ref
  126.9 0.6 copy-done.4
  127.6 1.0 copy-done.17
  128.6 9.9 %local_adjoint.1 = bf16[32,64,128]{2,1,0:T(8,128)(2,1)} custom-call(s32[48,3]{1,0:T(8,128)S(1)} %fusion.11.rows_ref, f32[48,3,256]{2,1,0:T(4,128)S(1)} %pad_convert_fusion.taps_ref, bf16[48,96,128]{2,1,0:T(8,128)(2,1)S(1)} %copy-done.4, bf16[32,64,128]{2,1,0:T(8,128)(2,1)S(1)} %copy-done.17, bf16[32,64,128]{2,1,0:T(8,128)(2,1)S(1)} %bitcast.26, ...), custom_call_target="tpu_custom_call" | custom-call | tf_op jit(solution)/shard_map/local_adjoint/pallas_call | solution.py:689
  (15 shorter events, 0.2 us)
Async XLA Ops:
  7.0 1.6 %copy-start = (bf16[32,2,128,128]{3,2,1,0:T(8,128)(2,1)S(1)}, bf16[32,2,128,128]{3,2,1,0:T(8,128)(2,1)}, u32[]{:S(2)}) copy-start(bf16[32,2,128,128]{3,2,1,0:T(8,128)(2,1)} %mix_ref.3) | copy-start | bytes 6291460
  8.6 0.9 copy-start.7
  9.5 0.9 copy-start.9
  10.5 1.0 copy-start.11
  11.5 51.6 %copy-start.21 = (s32[256,3]{0,1:T(4,128)S(1)}, s32[256,3]{0,1:T(4,128)}, u32[]{:S(2)}) copy-start(s32[256,3]{0,1:T(4,128)} %param.11) | copy-start | bytes 9220
  11.5 51.7 %copy-start.19 = (bf16[3,256,3,17]{1,2,3,0:T(4,128)(2,1)S(1)}, bf16[3,256,3,17]{1,2,3,0:T(4,128)(2,1)}, u32[]{:S(2)}) copy-start(bf16[3,256,3,17]{1,2,3,0:T(4,128)(2,1)} %param.10) | copy-start | bytes 235012
  61.2 1.0 copy-start.5
  62.3 0.8 copy-start.12
  63.1 1.0 copy-start.2
  63.1 1.0 copy-start.18
  63.6 12.1 %copy-start.10 = (bf16[2,256,256]{2,1,0:T(8,128)(2,1)S(1)}, bf16[2,256,256]{2,1,0:T(8,128)(2,1)}, u32[]{:S(2)}) copy-start(bf16[2,256,256]{2,1,0:T(8,128)(2,1)} %get-tuple-element.11.up_ref.down_ref) | copy-start | bytes 786436
  64.1 1.3 copy-start.6
  65.4 1.0 copy-start.13
  66.4 9.3 %copy-start.1 = (bf16[32,2,128,128]{3,2,1,0:T(8,128)(2,1)S(1)}, bf16[32,2,128,128]{3,2,1,0:T(8,128)(2,1)}, u32[]{:S(2)}) copy-start(bf16[32,2,128,128]{3,2,1,0:T(8,128)(2,1)} %mix_ref.3) | copy-start | bytes 6291460
  66.4 9.3 %copy-start.8 = (bf16[2,256,256]{2,1,0:T(8,128)(2,1)S(1)}, bf16[2,256,256]{2,1,0:T(8,128)(2,1)}, u32[]{:S(2)}) copy-start(bf16[2,256,256]{2,1,0:T(8,128)(2,1)} %get-tuple-element.10.down_ref.up_ref) | copy-start | bytes 786436
  74.9 0.8 copy-start.14
  75.8 1.0 copy-start.15
  76.8 49.5 %copy-start.20 = (bf16[3,256,3,17]{1,2,3,0:T(4,128)(2,1)S(1)}, bf16[3,256,3,17]{1,2,3,0:T(4,128)(2,1)}, u32[]{:S(2)}) copy-start(bf16[3,256,3,17]{1,2,3,0:T(4,128)(2,1)} %param.10) | copy-start | bytes 235012
  124.5 1.0 copy-start.3
  125.5 0.8 copy-start.16
  126.3 1.3 copy-start.4
  127.6 1.0 copy-start.17

commit v3 on v0

v3 whole, which is shorter than its diff:
```python
import functools
import math

import jax
import jax.numpy as jnp
from jax import lax
from jax.experimental import pallas as pl
from jax.experimental.pallas import tpu as pltpu
from jax.sharding import PartitionSpec as P

MDEV = 16
HW = 8


TANH_SCALE = 0.7978845608028654
CUBIC_TERM = 0.044715


def gelu_parts(values):
    tanh_input = TANH_SCALE * (values + CUBIC_TERM * values * values * values)
    hyper = jnp.tanh(tanh_input)
    result = 0.5 * values * (1.0 + hyper)
    derivative = 0.5 * (1.0 + hyper) + 0.5 * values * (1.0 - hyper * hyper) * TANH_SCALE * (
        1.0 + 3.0 * CUBIC_TERM * values * values
    )
    return (result, derivative)


def mode_tables(lon_count, mode_count):
    angles_int = (
        jnp.arange(lon_count, dtype=jnp.int32)[:, None]
        * jnp.arange(mode_count, dtype=jnp.int32)[None, :]
        % lon_count
    )
    angles = angles_int.astype(jnp.float32) * (2.0 * math.pi / lon_count)
    stacked = jnp.stack([jnp.cos(angles), -jnp.sin(angles)], axis=1)
    orders = jnp.arange(mode_count, dtype=jnp.int32)
    factor = jnp.where(orders == 0, 1.0, 2.0).astype(jnp.float32)
    to_modes = (stacked * (2.0 * math.pi / lon_count)).astype(jnp.bfloat16)
    from_modes = (stacked * factor[None, None, :]).astype(jnp.bfloat16)
    return (to_modes, from_modes)


STEP = 16


def legendre_kernel(gain_ref, back_ref, orders_ref, trig_ref, weighted_ref, plain_ref):
    order_share, degree_count, _ = plain_ref.shape
    cosine = trig_ref[0:1, :]
    quadrature = trig_ref[1:2, :]

    def block(index, state):
        carried = []
        for e in range(order_share):
            value, previous, log_scale = state[3 * e : 3 * e + 3]
            order = orders_ref[e]
            rows = []
            for step in range(STEP):
                degree = index * STEP + step
                active = degree > order
                following = gain_ref[e, degree] * (cosine * value) - back_ref[e, degree] * previous
                previous = jnp.where(active, value, previous)
                value = jnp.where(active, following, value)
                rows.append(jnp.where(degree >= order, value, 0.0))
            stacked = jnp.concatenate(rows, axis=0) * jnp.exp(log_scale)
            place = pl.ds(pl.multiple_of(index * STEP, STEP), STEP)
            plain_ref[e, place, :] = stacked.astype(jnp.bfloat16)
            weighted_ref[e, place, :] = (stacked * quadrature).astype(jnp.bfloat16)
            largest = jnp.maximum(jnp.abs(value), jnp.abs(previous))
            carried += [value / largest, previous / largest, log_scale + jnp.log(largest)]
        return tuple(carried)

    start = []
    for e in range(order_share):
        seed = trig_ref[2 + e : 3 + e, :]
        start += [jnp.ones_like(seed), jnp.zeros_like(seed), seed]
    lax.fori_loop(0, degree_count // STEP, block, tuple(start))


def legendre_inputs(orders, degree_count, lat_count):
    order_share = orders.shape[0]
    colatitude = math.pi * (jnp.arange(lat_count, dtype=jnp.float32) + 0.5) / lat_count
    sine_part = jnp.sin(colatitude)
    order_real = orders.astype(jnp.float32)
    seed_log = 0.5 * (
        jnp.log((2.0 * order_real + 1.0) / (4.0 * math.pi))
        + lax.lgamma(order_real + 0.5)
        - lax.lgamma(order_real + 1.0)
        - 0.5 * math.log(math.pi)
    )
    seed_log = seed_log[:, None] + order_real[:, None] * jnp.log(sine_part)[None, :]
    degree_real = jnp.arange(degree_count, dtype=jnp.float32)[None, :]
    order_row = order_real[:, None]
    forward_gain = jnp.sqrt(
        jnp.maximum(4.0 * degree_real * degree_real - 1.0, 1.0)
        / jnp.maximum(degree_real * degree_real - order_row * order_row, 1.0)
    )
    backward_gain = jnp.sqrt(
        jnp.maximum((degree_real - 1.0) ** 2 - order_row * order_row, 0.0)
        / jnp.maximum(4.0 * (degree_real - 1.0) ** 2 - 1.0, 1.0)
    )
    trig = jnp.concatenate(
        [
            jnp.cos(colatitude)[None, :],
            (math.pi / lat_count * sine_part)[None, :],
            seed_log,
        ],
        axis=0,
    )
    return (forward_gain, forward_gain * backward_gain, trig)


CHUNKS = 2
EDGE = 2 * HW


def place_of(lat_count, lon_count):
    lat_me = lax.axis_index("lat")
    lon_me = lax.axis_index("lon")
    return lat_me, lon_me


def enter(lat_count, lon_count):
    lat_me, lon_me = place_of(lat_count, lon_count)
    barrier = pltpu.get_barrier_semaphore()

    def greet(lat, lon):
        pl.semaphore_signal(
            barrier, inc=1, device_id=(lat, lon), device_id_type=pl.DeviceIdType.MESH
        )

    for step in range(1, lat_count):
        greet(lax.rem(lat_me + step, lat_count), lon_me)
    for step in range(1, lon_count):
        greet(lat_me, lax.rem(lon_me + step, lon_count))
    for lat_step in (1, lat_count - 1):
        for lon_step in (1, lon_count - 1):
            greet(lax.rem(lat_me + lat_step, lat_count), lax.rem(lon_me + lon_step, lon_count))
    return lambda: pl.semaphore_wait(barrier, lat_count - 1 + lon_count - 1 + 4)


def spectral_pass(
    lat_count,
    lon_count,
    adjoint,
    started,
    data_ref,
    first_ref,
    down_ref,
    up_ref,
    last_ref,
    mix_ref,
    padded_ref,
    part_out,
    pair_in,
    pair_out,
    cross_in,
    rows_out,
    rows_in,
    deg_out,
    deg_in,
    mixed_out,
    mixed_in,
    zonal_out,
    zonal_in,
    grid_out,
    grid_in,
    blended,
    pair_sems,
    cross_sems,
    lat_sems,
    gather_sems,
    relay_sems,
    halo_sems,
):
    row_count, lon_dev, channels = data_ref.shape
    order_share = down_ref.shape[0]
    degree_dev = mix_ref.shape[0]
    wide = 2 * channels
    share = lat_count * order_share
    modes = 2 * share
    chips = lon_count // 2
    rows_each = row_count // CHUNKS
    degrees_each = degree_dev // CHUNKS
    lat_me = lax.axis_index("lat")
    lon_me = lax.axis_index("lon")
    chip = lon_me // 2
    core = lax.rem(lon_me, 2)
    mate = 2 * chip + 1 - core
    lat_peers = [lax.rem(lat_me + step, lat_count) for step in range(1, lat_count)]
    chip_peers = [lax.rem(chip + step, chips) for step in range(1, chips)]
    lat_next = lax.rem(lat_me + 1, lat_count)
    lat_last = lax.rem(lat_me + lat_count - 1, lat_count)
    lon_next = lax.rem(lon_me + 1, lon_count)
    lon_last = lax.rem(lon_me + lon_count - 1, lon_count)
    halo_rows = {
        0: (lat_me, slice(0, row_count), slice(HW, HW + row_count)),
        1: (lat_next, slice(row_count - HW, row_count), slice(0, HW)),
        2: (lat_last, slice(0, HW), slice(HW + row_count, 2 * HW + row_count)),
    }
    halo_columns = {
        0: (lon_me, slice(0, lon_dev), slice(EDGE, EDGE + lon_dev)),
        1: (lon_next, slice(lon_dev - EDGE, lon_dev), slice(0, EDGE)),
        2: (lon_last, slice(0, EDGE), slice(EDGE + lon_dev, 2 * EDGE + lon_dev)),
    }

    def copying(source, target, sems, place, came, device):
        return pltpu.make_async_remote_copy(
            src_ref=source,
            dst_ref=target,
            send_sem=sems.at[(0,) + place],
            recv_sem=sems.at[(1,) + came],
            device_id=device,
            device_id_type=pl.DeviceIdType.MESH,
        )

    def push(source, target, sems, place, came, device):
        copy = copying(source, target, sems, place, came, device)
        copy.start()
        started.append(copy)

    def arrived(target, sems, came):
        copying(target, target, sems, came, came, (lat_me, mate)).wait_recv()

    def rows_of(number):
        return pl.ds(number * rows_each, rows_each)

    def transform(number):
        group = 8

        def body(index, carry):
            for step in range(group):
                row = number * rows_each + index * group + step
                part = jnp.dot(
                    first_ref[...], data_ref[row], preferred_element_type=jnp.float32
                ).astype(jnp.bfloat16)
                for other in range(chips):
                    for side in range(2):
                        begin = (2 * other + side) * modes
                        part_out[side, other, row] = part[begin : begin + modes]
            return carry

        lax.fori_loop(0, rows_each // group, body, 0)

    def lat_push(number, piece, source, target):
        for peer in lat_peers:
            push(
                source(peer),
                target(lat_me),
                lat_sems,
                (number, piece, peer),
                (number, piece, lat_me),
                (peer, lon_me),
            )

    def lat_arrived(number, piece, target):
        for peer in lat_peers:
            arrived(target(peer), lat_sems, (number, piece, peer))

    def begin(number):
        transform(number)

    def send(number):
        push(
            part_out.at[1 - core, :, rows_of(number)],
            pair_in.at[:, rows_of(number)],
            pair_sems,
            (number,),
            (number,),
            (lat_me, mate),
        )

    def halos_arrived():
        for r, (_, _, to_rows) in halo_rows.items():
            for c, (_, _, to_columns) in halo_columns.items():
                if r or c:
                    arrived(padded_ref.at[to_rows, to_columns], halo_sems, (3 * r + c,))

    def run(fill, finish, follow):
        for r, (lat, from_rows, to_rows) in halo_rows.items():
            for c, (lon, from_columns, to_columns) in halo_columns.items():
                if r or c:
                    push(
                        data_ref.at[from_rows, from_columns],
                        padded_ref.at[to_rows, to_columns],
                        halo_sems,
                        (3 * r + c,),
                        (3 * r + c,),
                        (lat, lon),
                    )
        for number in range(CHUNKS):
            piece = rows_of(number)
            arrived(pair_in.at[:, piece], pair_sems, (number,))
            for other in chip_peers:
                pair_out[other, piece] = (
                    part_out[core, other, piece].astype(jnp.float32)
                    + pair_in[other, piece].astype(jnp.float32)
                ).astype(jnp.bfloat16)
                push(
                    pair_out.at[other, piece],
                    cross_in.at[chip, piece],
                    cross_sems,
                    (number, other),
                    (number, chip),
                    (lat_me, 2 * other + core),
                )
        padded_ref[HW : HW + row_count, EDGE : EDGE + lon_dev] = data_ref[...]
        fill(0)
        for number in range(CHUNKS):
            piece = rows_of(number)
            total = part_out[core, chip, piece].astype(jnp.float32) + pair_in[chip, piece].astype(
                jnp.float32
            )
            for other in chip_peers:
                arrived(cross_in.at[other, piece], cross_sems, (number, other))
                total = total + cross_in[other, piece].astype(jnp.float32)
            begin = number * rows_each
            rows_out[:, :, :, begin : begin + rows_each] = (
                jnp.swapaxes(total, 0, 1)
                .astype(jnp.bfloat16)
                .reshape(lat_count, order_share, 2, rows_each, channels)
            )
            lat_push(
                0,
                number,
                lambda peer: rows_out.at[peer, :, :, piece],
                lambda peer: rows_in.at[peer, :, :, piece],
            )
        rows_in[lat_me] = rows_out[lat_me]
        fill(1)
        for number in range(CHUNKS):
            piece = rows_of(number)
            lat_arrived(0, number, lambda peer: rows_in.at[peer, :, :, piece])

        for e in range(order_share):
            columns = jnp.concatenate(
                [rows_in[:, e, part].reshape(lat_count * row_count, channels) for part in range(2)],
                axis=1,
            )
            degrees = jnp.dot(down_ref[e], columns, preferred_element_type=jnp.float32)
            deg_out[:, e] = degrees.astype(jnp.bfloat16).reshape(lat_count, degree_dev, wide)
        for number in range(CHUNKS):
            piece = pl.ds(number * degrees_each, degrees_each)
            lat_push(
                1,
                number,
                lambda peer: deg_out.at[peer, :, piece],
                lambda peer: deg_in.at[peer, :, piece],
            )
        deg_in[lat_me] = deg_out[lat_me]
        fill(2)

        for number in range(CHUNKS):
            begin = number * degrees_each
            piece = pl.ds(begin, degrees_each)
            lat_arrived(1, number, lambda peer: deg_in.at[peer, :, piece])
            by_degree = deg_in[:, :, begin : begin + degrees_each].reshape(share, degrees_each, wide)
            turned = jnp.swapaxes(by_degree.astype(jnp.float32), 0, 1).astype(jnp.bfloat16)
            for step in range(degrees_each):
                degree = begin + step
                pair = jnp.concatenate([turned[step, :, :channels], turned[step, :, channels:]], axis=0)
                if adjoint:
                    weights = jnp.concatenate([mix_ref[degree, 0], mix_ref[degree, 1]], axis=0)
                    product = lax.dot_general(
                        pair, weights, (((1,), (1,)), ((), ())), preferred_element_type=jnp.float32
                    )
                else:
                    weights = jnp.concatenate([mix_ref[degree, 0], mix_ref[degree, 1]], axis=1)
                    product = jnp.dot(pair, weights, preferred_element_type=jnp.float32)
                sign = -1.0 if adjoint else 1.0
                blended[step, :, :channels] = (
                    product[:share, :channels] - sign * product[share:, channels:]
                )
                blended[step, :, channels:] = (
                    sign * product[:share, channels:] + product[share:, :channels]
                )
            mixed_out[:, :, begin : begin + degrees_each] = (
                jnp.swapaxes(blended[...], 0, 1)
                .astype(jnp.bfloat16)
                .reshape(lat_count, order_share, degrees_each, wide)
            )
            lat_push(
                2,
                number,
                lambda peer: mixed_out.at[peer, :, piece],
                lambda peer: mixed_in.at[peer, :, piece],
            )
        mixed_in[lat_me] = mixed_out[lat_me]
        fill(3)
        for number in range(CHUNKS):
            piece = pl.ds(number * degrees_each, degrees_each)
            lat_arrived(2, number, lambda peer: mixed_in.at[peer, :, piece])

        for e in range(order_share):
            spectrum = mixed_in[:, e].reshape(lat_count * degree_dev, wide)
            zonal = lax.dot_general(
                up_ref[e], spectrum, (((0,), (0,)), ((), ())), preferred_element_type=jnp.float32
            ).astype(jnp.bfloat16)
            for part in range(2):
                zonal_out[:, e, part] = zonal[:, part * channels : (part + 1) * channels].reshape(
                    lat_count, row_count, channels
                )
        for number in range(CHUNKS):
            piece = rows_of(number)
            lat_push(
                3,
                number,
                lambda peer: zonal_out.at[peer, :, :, piece],
                lambda peer: zonal_in.at[peer, :, :, piece],
            )
        zonal_in[lat_me] = zonal_out[lat_me]
        fill(4)

        for number in range(CHUNKS):
            piece = rows_of(number)
            begin = number * rows_each
            lat_arrived(3, number, lambda peer: zonal_in.at[peer, :, :, piece])
            by_order = zonal_in[:, :, :, begin : begin + rows_each].reshape(modes, rows_each, channels)
            grid_out[piece] = jnp.swapaxes(by_order.astype(jnp.float32), 0, 1).astype(jnp.bfloat16)
            for lon in [2 * other + core for other in chip_peers] + [mate]:
                push(
                    grid_out.at[piece],
                    grid_in.at[lon_me, piece],
                    gather_sems,
                    (number, lon),
                    (number, lon_me),
                    (lat_me, lon),
                )
            grid_in[lon_me, piece] = grid_out[piece]
        fill(5)
        for number in range(CHUNKS):
            piece = rows_of(number)
            for other in chip_peers:
                slot = 2 * other + core
                arrived(grid_in.at[slot, piece], gather_sems, (number, slot))
                push(
                    grid_in.at[slot, piece],
                    grid_in.at[slot, piece],
                    relay_sems,
                    (number, slot),
                    (number, slot),
                    (lat_me, mate),
                )
        for number in range(CHUNKS):
            piece = rows_of(number)
            arrived(grid_in.at[mate, piece], gather_sems, (number, mate))
            for other in chip_peers:
                slot = 2 * other + 1 - core
                arrived(grid_in.at[slot, piece], relay_sems, (number, slot))

            def restore(index, carry):
                for step in range(8):
                    row = number * rows_each + index * 8 + step
                    every = grid_in[:, row].reshape(lon_count * modes, channels)
                    finish(
                        row,
                        jnp.dot(last_ref[...], every, preferred_element_type=jnp.float32)
                        .astype(jnp.bfloat16)
                        .astype(jnp.float32),
                    )
                return carry

            lax.fori_loop(0, rows_each // 8, restore, 0)
            follow(number)


    return begin, send, run, halos_arrived


def toeplitz(taps, count):
    spread = [
        pltpu.roll(
            jnp.broadcast_to(taps[k : k + 1, :], (count, taps.shape[1])),
            0,
            1,
            stride=1,
            stride_axis=0,
        )
        for k in range(taps.shape[0])
    ]
    return jnp.concatenate(spread, axis=0).astype(jnp.bfloat16)


def stretch(padded_ref, whole_ref):
    width = whole_ref.shape[1]

    def body(row, carry):
        whole_ref[row] = padded_ref[row].astype(jnp.float32)[HW : HW + width]
        return carry

    lax.fori_loop(0, whole_ref.shape[0], body, 0)


def whole_kernel(
    lat_count,
    lon_count,
    gain_ref,
    back_ref,
    orders_ref,
    sources_ref,
    near_ref,
    trig_ref,
    fields_ref,
    to_rows_ref,
    to_ref,
    from_rows_ref,
    from_ref,
    taps_ref,
    back_taps_ref,
    weight_ref,
    turned_weight_ref,
    cotangent_any,
    mix_any,
    out_ref,
    grad_ref,
    weighted,
    plain,
    mix,
    cotangent,
    padded,
    grad_padded,
    whole,
    conv,
    grad_mix,
    pieces,
    load_sems,
    *scratch,
):
    row_count, lon_dev, channels = fields_ref.shape
    tall, width, _ = whole.shape
    kernel_count = taps_ref.shape[1]
    band_count = sources_ref.shape[1]
    lanes = taps_ref.shape[2]
    wait_entry = enter(lat_count, lon_count)
    mix_load = pltpu.make_async_copy(mix_any, mix, load_sems.at[0])
    cotangent_load = pltpu.make_async_copy(cotangent_any, cotangent, load_sems.at[1])
    mix_load.start()
    cotangent_load.start()
    started = []
    half = len(scratch) // 2
    begin, send, run, halos = spectral_pass(
        lat_count,
        lon_count,
        False,
        started,
        fields_ref,
        to_rows_ref,
        weighted,
        plain,
        from_ref,
        mix,
        padded,
        *scratch[:half],
    )
    begin_back, send_back, run_back, halos_back = spectral_pass(
        lat_count,
        lon_count,
        True,
        started,
        grad_mix,
        from_rows_ref,
        plain,
        weighted,
        to_ref,
        mix,
        grad_padded,
        *scratch[half:],
    )

    def local_rows(first):
        def one(row):
            spare = jnp.zeros((lanes - band_count * width, channels), jnp.float32)
            sources = jnp.concatenate(
                [whole[sources_ref[row, band]] for band in range(band_count)] + [spare], axis=0
            ).astype(jnp.bfloat16)
            terms = jnp.dot(
                toeplitz(taps_ref[row], lon_dev), sources, preferred_element_type=jnp.float32
            ).astype(jnp.bfloat16)
            flat = jnp.concatenate(
                [terms[k * lon_dev : (k + 1) * lon_dev] for k in range(kernel_count)], axis=1
            )
            conv[row] = jnp.dot(flat, weight_ref[...], preferred_element_type=jnp.float32)

        def body(index, carry):
            for step in range(4):
                one(first + 4 * index + step)
            return carry

        lax.fori_loop(0, row_count // 16, body, 0)

    def fill(point):
        if point == 0:
            legendre_kernel(gain_ref, back_ref, orders_ref, trig_ref, weighted, plain)
        if point == 1:
            halos()
            stretch(padded, whole)
        if point == 2:
            mix_load.wait()
        if 1 <= point <= 4:
            local_rows((point - 1) * (row_count // 4))

    def finish(row, spectral):
        activation, derivative = gelu_parts(spectral + conv[row])
        out_ref[row] = (fields_ref[row].astype(jnp.float32) + activation).astype(jnp.bfloat16)
        grad_mix[row] = (cotangent[row].astype(jnp.float32) * derivative).astype(jnp.bfloat16)

    def follow(number):
        begin_back(number)
        send_back(number)

    for number in range(CHUNKS):
        begin(number)
        if number == 0:
            wait_entry()
        send(number)
    cotangent_load.wait()
    run(fill, finish, follow)

    def adjoint_rows(first):
        def one(row):
            spare = jnp.zeros((lanes - kernel_count * width, channels), jnp.bfloat16)
            grads = jnp.dot(
                whole[row].astype(jnp.bfloat16),
                turned_weight_ref[...],
                preferred_element_type=jnp.float32,
            ).astype(jnp.bfloat16)
            stacked = jnp.concatenate(
                [grads[:, k * channels : (k + 1) * channels] for k in range(kernel_count)] + [spare],
                axis=0,
            )
            spread = jnp.dot(
                toeplitz(back_taps_ref[row], lon_dev), stacked, preferred_element_type=jnp.float32
            )
            for band in range(band_count):
                pieces[row, band] = spread[band * lon_dev : (band + 1) * lon_dev]

        def body(index, carry):
            for step in range(4):
                one(first + 4 * index + step)
            return carry

        lax.fori_loop(0, tall // 16, body, 0)

    def gathered(row, full_first, full_last):
        total = cotangent[row].astype(jnp.float32)
        for band in range(band_count):
            offsets = range(2 * HW + 1)
            if band == 0 and not full_first:
                offsets = [2 * HW]
            if band == band_count - 1 and not full_last:
                offsets = [0]
            for offset in offsets:
                hit = near_ref[row + offset, band] == row
                total = total + jnp.where(hit, 1.0, 0.0) * pieces[row + offset, band]
        conv[row] = total

    def fill_back(point):
        if point == 1:
            halos_back()
            stretch(grad_padded, whole)
        if 1 <= point <= 4:
            adjoint_rows((point - 1) * (tall // 4))
        if point == 5:
            gathered(0, True, False)
            gathered(row_count - 1, False, True)

            def body(row, carry):
                gathered(row, False, False)
                return carry

            lax.fori_loop(1, row_count - 1, body, 0)

    def finish_back(row, spectral):
        grad_ref[row] = (conv[row] + spectral).astype(jnp.bfloat16)

    run_back(fill_back, finish_back, lambda number: None)
    for copy in started:
        copy.wait_send()


def pass_scratch(lat_count, lon_count, row_count, order_share, degree_dev, channels):
    share = lat_count * order_share
    wide = 2 * channels
    chips = lon_count // 2
    bf16 = jnp.bfloat16
    part = pltpu.VMEM((chips, row_count, 2 * share, channels), bf16)
    rows = pltpu.VMEM((lat_count, order_share, 2, row_count, channels), bf16)
    degrees = pltpu.VMEM((lat_count, order_share, degree_dev, wide), bf16)
    return [
        pltpu.VMEM((2, chips, row_count, 2 * share, channels), bf16),
        part,
        part,
        part,
        rows,
        rows,
        degrees,
        degrees,
        degrees,
        degrees,
        rows,
        rows,
        pltpu.VMEM((row_count, 2 * share, channels), bf16),
        pltpu.VMEM((lon_count, row_count, 2 * share, channels), bf16),
        pltpu.VMEM((degree_dev // CHUNKS, share, wide), jnp.float32),
        pltpu.SemaphoreType.DMA((2, CHUNKS)),
        pltpu.SemaphoreType.DMA((2, CHUNKS, chips)),
        pltpu.SemaphoreType.DMA((2, 4, CHUNKS, lat_count)),
        pltpu.SemaphoreType.DMA((2, CHUNKS, lon_count)),
        pltpu.SemaphoreType.DMA((2, CHUNKS, lon_count)),
        pltpu.SemaphoreType.DMA((2, 9)),
    ]


def tap_rows(basis, width):
    flat = jnp.pad(basis, ((0, 0), (0, 0), (0, 0), (0, width - basis.shape[3])))
    flat = flat.reshape(basis.shape[0], basis.shape[1], basis.shape[2] * width)
    lanes = -(-flat.shape[2] // 128) * 128
    return jnp.pad(flat, ((0, 0), (0, 0), (0, lanes - flat.shape[2]))).astype(jnp.float32)


def per_device(fields, cotangent, spectral_weight, local_weight, filter_basis, neighbor_rows):
    lat_count = lax.axis_size("lat")
    lon_count = lax.axis_size("lon")
    lat_index = lax.axis_index("lat")
    lon_index = lax.axis_index("lon")
    _, lat_dev, lon_dev, channels = fields.shape
    degree_dev = spectral_weight.shape[0]
    kernel_count = filter_basis.shape[0]
    total_lat = lat_dev * lat_count
    total_lon = lon_dev * lon_count
    order_share = MDEV // lat_count
    width = lon_dev + 2 * HW
    tall = lat_dev + 2 * HW
    to_modes, from_modes = mode_tables(total_lon, MDEV * lon_count)
    table_shape = (lon_dev, 2, lon_count, lat_count, order_share)
    to_modes = lax.dynamic_slice_in_dim(to_modes, lon_index * lon_dev, lon_dev, 0)
    from_modes = lax.dynamic_slice_in_dim(from_modes, lon_index * lon_dev, lon_dev, 0)
    to_modes = to_modes.reshape(table_shape).transpose(0, 2, 3, 4, 1).reshape(lon_dev, -1)
    from_modes = from_modes.reshape(table_shape).transpose(0, 2, 3, 4, 1).reshape(lon_dev, -1)
    orders = (
        lon_index * MDEV + lat_index * order_share + jnp.arange(order_share, dtype=jnp.int32)
    )
    gain, back_gain, trig = legendre_inputs(orders, degree_dev * lat_count, total_lat)
    row_base = lat_index * lat_dev
    near_rows = lax.dynamic_slice_in_dim(
        jnp.pad(neighbor_rows, ((HW, HW), (0, 0))), row_base, tall, 0
    )
    near_basis = lax.dynamic_slice_in_dim(
        jnp.pad(filter_basis, ((0, 0), (HW, HW), (0, 0), (0, 0))), row_base, tall, 1
    )
    sources = near_rows[HW : HW + lat_dev] - row_base + HW
    taps = tap_rows(near_basis[:, HW : HW + lat_dev].transpose(1, 0, 2, 3), width)
    back_taps = tap_rows(near_basis[..., ::-1].transpose(1, 2, 0, 3), width)
    smem = pl.BlockSpec(memory_space=pltpu.SMEM)
    vmem = pl.BlockSpec(memory_space=pltpu.VMEM)
    grid = jax.ShapeDtypeStruct((lat_dev, lon_dev, channels), jnp.bfloat16)
    bf16 = jnp.bfloat16
    table = pltpu.VMEM((order_share, degree_dev * lat_count, total_lat), bf16)
    rim = pltpu.VMEM((tall, lon_dev + 2 * EDGE, channels), bf16)
    passes = pass_scratch(lat_count, lon_count, lat_dev, order_share, degree_dev, channels)
    block_output, input_grad = pl.pallas_call(
        functools.partial(whole_kernel, lat_count, lon_count),
        out_shape=(grid, grid),
        in_specs=[smem] * 5 + [vmem] * 10 + [pl.BlockSpec(memory_space=pl.ANY)] * 2,
        out_specs=(vmem, vmem),
        scratch_shapes=[
            table,
            table,
            pltpu.VMEM(spectral_weight.shape, bf16),
            pltpu.VMEM((lat_dev, lon_dev, channels), bf16),
            rim,
            rim,
            pltpu.VMEM((tall, width, channels), jnp.float32),
            pltpu.VMEM((lat_dev, lon_dev, channels), jnp.float32),
            pltpu.VMEM((lat_dev, lon_dev, channels), bf16),
            pltpu.VMEM((tall, filter_basis.shape[2], lon_dev, channels), jnp.float32),
            pltpu.SemaphoreType.DMA((2,)),
        ]
        + passes
        + passes,
        compiler_params=pltpu.CompilerParams(
            collective_id=0, has_side_effects=True, vmem_limit_bytes=56 * 1024 * 1024
        ),
        name="operator_block",
    )(
        gain,
        back_gain,
        orders,
        sources,
        near_rows - row_base,
        trig,
        fields[0],
        to_modes.T,
        to_modes,
        from_modes.T,
        from_modes,
        taps,
        back_taps,
        local_weight.reshape(-1, channels),
        local_weight.transpose(2, 0, 1).reshape(channels, kernel_count * channels),
        cotangent[0],
        spectral_weight,
    )
    return (block_output[None], input_grad[None])


def solution(mesh):
    in_specs = (
        P(None, "lat", "lon", None),
        P(None, "lat", "lon", None),
        P("lat", None, None, None),
        P(),
        P(),
        P(),
    )
    out_specs = (P(None, "lat", "lon", None), P(None, "lat", "lon", None))
    return jax.shard_map(
        per_device, mesh=mesh, in_specs=in_specs, out_specs=out_specs, check_vma=False
    )
```

time: 231 us -> 116 us (0.50)
  Pallas kernels: 3.62 us -> 98.9 us
  starting transfers between devices: 72.4 us -> 0 us
  matrix products: 62.7 us -> 0 us
  waiting for transfers between devices: 45.7 us -> 0 us
  local copies, waits for them, and re-layouts: 33.8 us -> 10.4 us
  other arithmetic: 9.73 us -> 5.13 us
    pallas_call x1, Pallas kernels: 3.62 us -> 98.9 us  [per_device(): pl.pallas_call(functools.partial(whole_kernel, lat_count, lon_count), out...]
    dot_general x26 -> x0, matrix products: 62.7 us -> none  [the longest x3 9.9 us: per_device(): jnp.einsum('ji,aiqc->ajqc', placing, spread, precision=lax.Precision.HIGH...]
    all_to_all x12 -> x0, starting transfers between devices: 58.5 us -> none  [swap(): return lax.all_to_all(blocks, axis, split_axis=0, concat_axis=0, tiled=True)]
    all_to_all x12 -> x0, waiting for transfers between devices: 42 us -> none  [swap(): return lax.all_to_all(blocks, axis, split_axis=0, concat_axis=0, tiled=True)]
    ppermute x8 -> x0, starting transfers between devices: 13.9 us -> none  [the longest x4 8.11 us: extended(): lax.ppermute(tail, axis, [(i, (i + 1) % count) for i in range(count)])]
    convert_element_type x8 -> x0, local copies, waits for them, and re-layouts: 7.95 us -> none  [the longest x2 2.61 us: analysis(): partial = jnp.einsum('ifc,fkjbe->jbekic', field_blocks, dft_table, prefer...]
    gather x5 -> x0, local copies, waits for them, and re-layouts: 5.78 us -> none  [the longest x3 4.44 us: per_device(): sources = jnp.take(padded, source_rows, axis=1)]
    reshape x4 -> x5, local copies, waits for them, and re-layouts: 7.66 us -> 3.33 us  [the longest x1 1.65 us: per_device(): local_weight.transpose(2, 0, 1).reshape(channels, kernel_count * channels)]
  transfers between devices with their start and end apart: 20 -> 0, of which waited for: 11 -> 0; matrix products, arithmetic and copies ran while one was open for 36% -> 0% of each run, Pallas kernels for 2% -> 0%
where the time goes in v3:
time: 116 us; the launch traced here: 115 us
  Pallas kernels  98.9 us (85%)
  local copies, waits for them, and re-layouts  10.4 us (9%)
  other arithmetic  5.13 us (4%)
    pallas_call x1, Pallas kernels, per_device(): pl.pallas_call(functools.partial(whole_kernel, lat_count, lon_count), out...  98.9 us
    unnamed x8, local copies, waits for them, and re-layouts  4.74 us

profile of v3, /device:TPU:1, one launch (start us, length us, event | category | flops | bytes accessed | tf_op | source)
XLA Modules:
  0.0 115.1 jit_solution(5853392537361170526)
XLA Ops:
  0.7 0.1 add_multiply_fusion.2
  0.8 0.5 iota_add_fusion
  1.3 0.1 multiply_add_fusion
  1.4 0.1 sine_multiply_fusion
  1.5 0.6 pad_maximum_fusion.trig_ref
  2.1 0.7 sqrt_multiply_fusion
  2.8 1.0 fusion.7
  3.8 0.2 copy.44
  4.0 0.1 pad.26.clone
  4.0 0.1 reshape.298
  4.2 1.0 pad_dynamic-slice_fusion.1
  5.2 0.7 pad_convert_fusion.1.taps_ref
  5.9 1.6 %copy.39.turned_weight_ref = bf16[128,384]{1,0:T(8,128)(2,1)} copy(bf16[128,384]{0,1:T(8,128)(2,1)} %bitcast.30) | data formatting | bytes 196608 | tf_op jit(solution)/shard_map/reshape | solution.py:800
  7.5 0.8 copy.30
  8.4 0.6 fusion.11.sources_ref
  9.0 0.6 fusion.9.near_ref
  9.6 0.3 sine_negate_fusion
  9.9 0.1 multiply_convert_fusion
  10.0 0.0 copy-start
  10.1 0.0 copy-start.1
  10.1 0.7 copy.37.to_ref
  10.8 0.7 copy.38.from_ref
  11.5 0.1 pad.28
  11.6 0.2 copy.36
  11.8 0.7 pad_convert_fusion.back_taps_ref
  12.5 0.0 copy-done
  12.5 0.0 copy-done.1
  12.5 98.9 %operator_block.1 = (bf16[32,64,128]{2,1,0:T(8,128)(2,1)}, bf16[32,64,128]{2,1,0:T(8,128)(2,1)}) custom-call(f32[2,256]{1,0:T(2,128)} %get-tuple-element.9.gain_ref, f32[2,256]{1,0:T(2,128)} %get-tuple-element.8.back_ref, s32[2]{0:T(128)} %get-tuple-element.12.orders_ref, s32[32,3]{1,0:T(8,128)} %fusion.11.sources_ref, s32[48,3]{1,0:T(8,128)} %fusion.9.near_ref, ...), custom_call_target="tpu_custom_call" | custom-call | tf_op jit(solution)/shard_map/operator_block/pallas_call | solution.py:761
  111.4 1.9 %copy.47 = bf16[1,32,64,128]{3,2,1,0:T(8,128)(2,1)} copy(bf16[1,32,64,128]{3,2,1,0:T(8,128)(2,1)} %bitcast.27) | data formatting | bytes 1048576
  113.2 1.9 %copy.48 = bf16[1,32,64,128]{3,2,1,0:T(8,128)(2,1)} copy(bf16[1,32,64,128]{3,2,1,0:T(8,128)(2,1)} %bitcast.26) | data formatting | bytes 1048576
  (7 shorter events, 0.2 us)
Async XLA Ops:
  10.0 2.4 %copy-start = (bf16[64,4,8,2,2]{0,4,3,2,1:T(2,128)(2,1)}, bf16[64,4,8,2,2]{0,4,3,2,1:T(2,128)(2,1)S(1)}, u32[]{:S(2)}) copy-start(bf16[64,4,8,2,2]{0,4,3,2,1:T(2,128)(2,1)S(1)} %copy.32) | copy-start | bytes 49156
  10.1 2.4 %copy-start.1 = (bf16[64,4,8,2,2]{0,4,3,2,1:T(2,128)(2,1)}, bf16[64,4,8,2,2]{0,4,3,2,1:T(2,128)(2,1)S(1)}, u32[]{:S(2)}) copy-start(bf16[64,4,8,2,2]{0,4,3,2,1:T(2,128)(2,1)S(1)} %copy.31) | copy-start | bytes 49156

commit v4 on v3

--- a/solution.py
+++ b/solution.py
@@ -497,18 +497,14 @@
     gain_ref,
     back_ref,
     orders_ref,
-    sources_ref,
     near_ref,
     trig_ref,
     fields_ref,
     to_rows_ref,
-    to_ref,
     from_rows_ref,
-    from_ref,
     taps_ref,
     back_taps_ref,
     weight_ref,
-    turned_weight_ref,
     cotangent_any,
     mix_any,
     out_ref,
@@ -523,13 +519,15 @@
     conv,
     grad_mix,
     pieces,
+    to_ref,
+    from_ref,
     load_sems,
     *scratch,
 ):
     row_count, lon_dev, channels = fields_ref.shape
     tall, width, _ = whole.shape
     kernel_count = taps_ref.shape[1]
-    band_count = sources_ref.shape[1]
+    band_count = near_ref.shape[1]
     lanes = taps_ref.shape[2]
     wait_entry = enter(lat_count, lon_count)
     mix_load = pltpu.make_async_copy(mix_any, mix, load_sems.at[0])
@@ -571,7 +569,7 @@
         def one(row):
             spare = jnp.zeros((lanes - band_count * width, channels), jnp.float32)
             sources = jnp.concatenate(
-                [whole[sources_ref[row, band]] for band in range(band_count)] + [spare], axis=0
+                [whole[near_ref[row + HW, band] + HW] for band in range(band_count)] + [spare], axis=0
             ).astype(jnp.bfloat16)
             terms = jnp.dot(
                 toeplitz(taps_ref[row], lon_dev), sources, preferred_element_type=jnp.float32
@@ -590,14 +588,16 @@
 
     def fill(point):
         if point == 0:
+            for rows_ref, columns_ref in ((to_rows_ref, to_ref), (from_rows_ref, from_ref)):
+                columns_ref[...] = rows_ref[...].astype(jnp.float32).T.astype(jnp.bfloat16)
+        if point == 1:
             legendre_kernel(gain_ref, back_ref, orders_ref, trig_ref, weighted, plain)
-        if point == 1:
             halos()
             stretch(padded, whole)
         if point == 2:
             mix_load.wait()
-        if 1 <= point <= 4:
-            local_rows((point - 1) * (row_count // 4))
+        if 2 <= point <= 5:
+            local_rows((point - 2) * (row_count // 4))
 
     def finish(row, spectral):
         activation, derivative = gelu_parts(spectral + conv[row])
@@ -616,12 +616,13 @@
     cotangent_load.wait()
     run(fill, finish, follow)
 
-    def adjoint_rows(first):
+    def adjoint_rows(first, count):
         def one(row):
             spare = jnp.zeros((lanes - kernel_count * width, channels), jnp.bfloat16)
-            grads = jnp.dot(
+            grads = lax.dot_general(
                 whole[row].astype(jnp.bfloat16),
-                turned_weight_ref[...],
+                weight_ref[...],
+                (((1,), (1,)), ((), ())),
                 preferred_element_type=jnp.float32,
             ).astype(jnp.bfloat16)
             stacked = jnp.concatenate(
@@ -639,7 +640,7 @@
                 one(first + 4 * index + step)
             return carry
 
-        lax.fori_loop(0, tall // 16, body, 0)
+        lax.fori_loop(0, count // 4, body, 0)
 
     def gathered(row, full_first, full_last):
         total = cotangent[row].astype(jnp.float32)
@@ -654,12 +655,20 @@
                 total = total + jnp.where(hit, 1.0, 0.0) * pieces[row + offset, band]
         conv[row] = total
 
+    quarter = tall // 4
+    shares = (
+        (0, quarter + 4),
+        (quarter + 4, quarter - 4),
+        (2 * quarter, quarter),
+        (3 * quarter, quarter),
+    )
+
     def fill_back(point):
         if point == 1:
             halos_back()
             stretch(grad_padded, whole)
         if 1 <= point <= 4:
-            adjoint_rows((point - 1) * (tall // 4))
+            adjoint_rows(*shares[point - 1])
         if point == 5:
             gathered(0, True, False)
             gathered(row_count - 1, False, True)
@@ -676,6 +685,11 @@
     run_back(fill_back, finish_back, lambda number: None)
     for copy in started:
         copy.wait_send()
+
+
+def settle_kernel(first_in, second_in, first_out, second_out):
+    first_out[...] = first_in[...]
+    second_out[...] = second_in[...]
 
 
 def pass_scratch(lat_count, lon_count, row_count, order_share, degree_dev, channels):
@@ -725,7 +739,6 @@
     lon_index = lax.axis_index("lon")
     _, lat_dev, lon_dev, channels = fields.shape
     degree_dev = spectral_weight.shape[0]
-    kernel_count = filter_basis.shape[0]
     total_lat = lat_dev * lat_count
     total_lon = lon_dev * lon_count
     order_share = MDEV // lat_count
@@ -748,7 +761,6 @@
     near_basis = lax.dynamic_slice_in_dim(
         jnp.pad(filter_basis, ((0, 0), (HW, HW), (0, 0), (0, 0))), row_base, tall, 1
     )
-    sources = near_rows[HW : HW + lat_dev] - row_base + HW
     taps = tap_rows(near_basis[:, HW : HW + lat_dev].transpose(1, 0, 2, 3), width)
     back_taps = tap_rows(near_basis[..., ::-1].transpose(1, 2, 0, 3), width)
     smem = pl.BlockSpec(memory_space=pltpu.SMEM)
@@ -761,7 +773,7 @@
     block_output, input_grad = pl.pallas_call(
         functools.partial(whole_kernel, lat_count, lon_count),
         out_shape=(grid, grid),
-        in_specs=[smem] * 5 + [vmem] * 10 + [pl.BlockSpec(memory_space=pl.ANY)] * 2,
+        in_specs=[smem] * 4 + [vmem] * 7 + [pl.BlockSpec(memory_space=pl.ANY)] * 2,
         out_specs=(vmem, vmem),
         scratch_shapes=[
             table,
@@ -774,6 +786,8 @@
             pltpu.VMEM((lat_dev, lon_dev, channels), jnp.float32),
             pltpu.VMEM((lat_dev, lon_dev, channels), bf16),
             pltpu.VMEM((tall, filter_basis.shape[2], lon_dev, channels), jnp.float32),
+            pltpu.VMEM(to_modes.shape, bf16),
+            pltpu.VMEM(to_modes.shape, bf16),
             pltpu.SemaphoreType.DMA((2,)),
         ]
         + passes
@@ -786,21 +800,27 @@
         gain,
         back_gain,
         orders,
-        sources,
         near_rows - row_base,
         trig,
         fields[0],
         to_modes.T,
-        to_modes,
         from_modes.T,
-        from_modes,
         taps,
         back_taps,
         local_weight.reshape(-1, channels),
-        local_weight.transpose(2, 0, 1).reshape(channels, kernel_count * channels),
         cotangent[0],
         spectral_weight,
     )
+    quarter = pl.BlockSpec((lat_dev // 4, lon_dev, channels), lambda index: (index, 0, 0))
+    block_output, input_grad = pl.pallas_call(
+        settle_kernel,
+        grid=(4,),
+        out_shape=(grid, grid),
+        in_specs=[quarter] * 2,
+        out_specs=(quarter, quarter),
+        compiler_params=pltpu.CompilerParams(vmem_limit_bytes=56 * 1024 * 1024),
+        name="settle",
+    )(block_output, input_grad)
     return (block_output[None], input_grad[None])
 
 

time: 116 us -> 111 us (0.957)
  local copies, waits for them, and re-layouts: 10.4 us -> 4.79 us
  Pallas kernels: 98.9 us -> 101 us
    unnamed x8 -> x2, local copies, waits for them, and re-layouts: 4.74 us -> 0.99 us
    pallas_call x0 -> x1, Pallas kernels: none -> 3.41 us  [per_device(): pl.pallas_call(settle_kernel, grid=(4,), out_shape=(grid, grid), in_specs...]
    reshape x3 -> x0, local copies, waits for them, and re-layouts: 3.02 us -> none  [the longest x1 1.65 us: per_device(): local_weight.transpose(2, 0, 1).reshape(channels, kernel_count * channels)]
    pallas_call x1, Pallas kernels: 98.9 us -> 97.6 us  [per_device(): pl.pallas_call(functools.partial(whole_kernel, lat_count, lon_count), out...]
where the time goes in v4:
time: 111 us
  Pallas kernels  101 us (91%)
  local copies, waits for them, and re-layouts  4.79 us (4%)
  other arithmetic  4.5 us (4%)
    pallas_call x1, Pallas kernels, per_device(): pl.pallas_call(functools.partial(whole_kernel, lat_count, lon_count), out...  97.6 us
    pallas_call x1, Pallas kernels, per_device(): pl.pallas_call(settle_kernel, grid=(4,), out_shape=(grid, grid), in_specs...  3.41 us

profile of v4, /device:TPU:1, one launch (start us, length us, event | category | flops | bytes accessed | tf_op | source)
XLA Modules:
  0.0 111.0 jit_solution(1088036938226777642)
XLA Ops:
  0.7 0.1 add_multiply_fusion.2
  0.8 0.5 iota_add_fusion
  1.3 0.1 multiply_add_fusion
  1.4 0.1 sine_multiply_fusion
  1.4 0.6 pad_maximum_fusion.trig_ref
  2.1 0.7 sqrt_multiply_fusion
  2.7 1.0 fusion.7
  3.8 0.2 copy.32
  3.9 0.1 pad.26.clone
  4.0 0.1 reshape.294
  4.1 1.0 pad_dynamic-slice_fusion.1
  5.2 0.7 pad_convert_fusion.1.taps_ref
  5.9 0.8 copy.21
  6.7 0.6 fusion.9.near_ref
  7.3 0.3 sine_negate_fusion
  7.6 0.1 multiply_convert_fusion
  7.7 0.6 copy.23
  8.4 0.6 copy.22
  9.0 0.1 pad.28
  9.1 0.2 copy.27
  9.3 0.7 pad_convert_fusion.back_taps_ref
  10.0 97.6 %operator_block.1 = (bf16[32,64,128]{2,1,0:T(8,128)(2,1)}, bf16[32,64,128]{2,1,0:T(8,128)(2,1)}) custom-call(f32[2,256]{1,0:T(2,128)} %get-tuple-element.13.gain_ref, f32[2,256]{1,0:T(2,128)} %get-tuple-element.12.back_ref, s32[2]{0:T(128)} %get-tuple-element.16.orders_ref, s32[48,3]{1,0:T(8,128)} %fusion.9.near_ref, f32[4,256]{1,0:T(4,128)} %pad_maximum_fusion.trig_ref, ...), custom_call_target="tpu_custom_call" | custom-call | tf_op jit(solution)/shard_map/operator_block/pallas_call | solution.py:773
  107.6 3.4 %settle.1 = (bf16[32,64,128]{2,1,0:T(8,128)(2,1)}, bf16[32,64,128]{2,1,0:T(8,128)(2,1)}) custom-call(bf16[32,64,128]{2,1,0:T(8,128)(2,1)} %get-tuple-element.6.first_in, bf16[32,64,128]{2,1,0:T(8,128)(2,1)} %get-tuple-element.7.second_in), custom_call_target="tpu_custom_call" | custom-call | tf_op jit(solution)/shard_map/settle/pallas_call | solution.py:815
  (5 shorter events, 0.1 us)

commit v5 on v4

--- a/solution.py
+++ b/solution.py
@@ -111,6 +111,7 @@
 
 
 CHUNKS = 2
+SUPPORT = 2 * HW + 1
 EDGE = 2 * HW
 
 
@@ -503,7 +504,6 @@
     to_rows_ref,
     from_rows_ref,
     taps_ref,
-    back_taps_ref,
     weight_ref,
     cotangent_any,
     mix_any,
@@ -526,9 +526,9 @@
 ):
     row_count, lon_dev, channels = fields_ref.shape
     tall, width, _ = whole.shape
-    kernel_count = taps_ref.shape[1]
+    kernel_count = weight_ref.shape[0] // channels
     band_count = near_ref.shape[1]
-    lanes = taps_ref.shape[2]
+    lanes = -(-max(kernel_count, band_count) * width // 128) * 128
     wait_entry = enter(lat_count, lon_count)
     mix_load = pltpu.make_async_copy(mix_any, mix, load_sems.at[0])
     cotangent_load = pltpu.make_async_copy(cotangent_any, cotangent, load_sems.at[1])
@@ -565,6 +565,25 @@
         *scratch[half:],
     )
 
+    def tap_lines(row, shift, line_count, block_count, line_stride, block_stride):
+        taps = taps_ref[row]
+        if shift:
+            taps = pltpu.roll(taps, taps.shape[1] - shift, 1)
+        lane = lax.broadcasted_iota(jnp.int32, taps.shape, 1)
+        taps = jnp.where(lane < SUPPORT, taps, 0.0)
+        taps = jnp.concatenate(
+            [taps, jnp.zeros((taps.shape[0], lanes - taps.shape[1]), jnp.float32)], axis=1
+        )
+        moved = [taps] + [pltpu.roll(taps, block * width, 1) for block in range(1, block_count)]
+        lines = []
+        for line in range(line_count):
+            total = 0.0
+            for block in range(block_count):
+                index = line * line_stride + block * block_stride
+                total = total + moved[block][index : index + 1]
+            lines.append(total)
+        return jnp.concatenate(lines, axis=0)
+
     def local_rows(first):
         def one(row):
             spare = jnp.zeros((lanes - band_count * width, channels), jnp.float32)
@@ -572,7 +591,7 @@
                 [whole[near_ref[row + HW, band] + HW] for band in range(band_count)] + [spare], axis=0
             ).astype(jnp.bfloat16)
             terms = jnp.dot(
-                toeplitz(taps_ref[row], lon_dev), sources, preferred_element_type=jnp.float32
+                toeplitz(tap_lines(row + HW, 0, kernel_count, band_count, band_count, 1), lon_dev), sources, preferred_element_type=jnp.float32
             ).astype(jnp.bfloat16)
             flat = jnp.concatenate(
                 [terms[k * lon_dev : (k + 1) * lon_dev] for k in range(kernel_count)], axis=1
@@ -630,7 +649,7 @@
                 axis=0,
             )
             spread = jnp.dot(
-                toeplitz(back_taps_ref[row], lon_dev), stacked, preferred_element_type=jnp.float32
+                toeplitz(tap_lines(row, SUPPORT, band_count, kernel_count, 1, band_count), lon_dev), stacked, preferred_element_type=jnp.float32
             )
             for band in range(band_count):
                 pieces[row, band] = spread[band * lon_dev : (band + 1) * lon_dev]
@@ -725,11 +744,13 @@
     ]
 
 
-def tap_rows(basis, width):
-    flat = jnp.pad(basis, ((0, 0), (0, 0), (0, 0), (0, width - basis.shape[3])))
-    flat = flat.reshape(basis.shape[0], basis.shape[1], basis.shape[2] * width)
-    lanes = -(-flat.shape[2] // 128) * 128
-    return jnp.pad(flat, ((0, 0), (0, 0), (0, lanes - flat.shape[2]))).astype(jnp.float32)
+def tap_rows(basis):
+    both = jnp.concatenate([basis, basis[..., ::-1]], axis=3).transpose(1, 0, 2, 3)
+    flat = both.reshape(both.shape[0], both.shape[1] * both.shape[2], both.shape[3])
+    rows = -(-flat.shape[1] // 8) * 8
+    return jnp.pad(
+        flat, ((0, 0), (0, rows - flat.shape[1]), (0, 128 - flat.shape[2]))
+    ).astype(jnp.float32)
 
 
 def per_device(fields, cotangent, spectral_weight, local_weight, filter_basis, neighbor_rows):
@@ -761,8 +782,7 @@
     near_basis = lax.dynamic_slice_in_dim(
         jnp.pad(filter_basis, ((0, 0), (HW, HW), (0, 0), (0, 0))), row_base, tall, 1
     )
-    taps = tap_rows(near_basis[:, HW : HW + lat_dev].transpose(1, 0, 2, 3), width)
-    back_taps = tap_rows(near_basis[..., ::-1].transpose(1, 2, 0, 3), width)
+    taps = tap_rows(near_basis)
     smem = pl.BlockSpec(memory_space=pltpu.SMEM)
     vmem = pl.BlockSpec(memory_space=pltpu.VMEM)
     grid = jax.ShapeDtypeStruct((lat_dev, lon_dev, channels), jnp.bfloat16)
@@ -773,7 +793,7 @@
     block_output, input_grad = pl.pallas_call(
         functools.partial(whole_kernel, lat_count, lon_count),
         out_shape=(grid, grid),
-        in_specs=[smem] * 4 + [vmem] * 7 + [pl.BlockSpec(memory_space=pl.ANY)] * 2,
+        in_specs=[smem] * 4 + [vmem] * 6 + [pl.BlockSpec(memory_space=pl.ANY)] * 2,
         out_specs=(vmem, vmem),
         scratch_shapes=[
             table,
@@ -806,7 +826,6 @@
         to_modes.T,
         from_modes.T,
         taps,
-        back_taps,
         local_weight.reshape(-1, channels),
         cotangent[0],
         spectral_weight,

time: 111 us -> 110 us (level)
  local copies, waits for them, and re-layouts: 4.79 us -> 3.41 us
where the time goes in v5:
time: 110 us
  Pallas kernels  102 us (93%)
  other arithmetic  3.91 us (4%)
  local copies, waits for them, and re-layouts  3.41 us (3%)
    pallas_call x1, Pallas kernels, per_device(): pl.pallas_call(functools.partial(whole_kernel, lat_count, lon_count), out...  98.4 us
    pallas_call x1, Pallas kernels, per_device(): pl.pallas_call(settle_kernel, grid=(4,), out_shape=(grid, grid), in_specs...  3.41 us

profile of v5, /device:TPU:1, one launch (start us, length us, event | category | flops | bytes accessed | tf_op | source)
XLA Modules:
  0.0 109.8 jit_solution(18292088797640902258)
XLA Ops:
  0.7 0.1 add_multiply_fusion.2
  0.8 0.5 iota_add_fusion
  1.3 0.1 multiply_add_fusion
  1.4 0.1 sine_multiply_fusion
  1.5 0.6 pad_maximum_fusion.1.trig_ref
  2.1 0.7 sqrt_multiply_fusion
  2.7 0.9 copy.19
  3.7 0.1 pad_dynamic-slice_fusion
  3.8 0.1 rev.3
  3.9 0.2 copy.20
  4.1 0.8 copy.16
  4.9 0.6 fusion.8.near_ref
  5.5 0.3 sine_negate_fusion
  5.8 0.1 multiply_convert_fusion
  5.9 0.6 copy.18
  6.6 0.6 copy.17
  7.2 0.8 pad_convert_fusion.taps_ref
  8.0 98.4 %operator_block.1 = (bf16[32,64,128]{2,1,0:T(8,128)(2,1)}, bf16[32,64,128]{2,1,0:T(8,128)(2,1)}) custom-call(f32[2,256]{1,0:T(2,128)} %get-tuple-element.13.gain_ref, f32[2,256]{1,0:T(2,128)} %get-tuple-element.12.back_ref, s32[2]{0:T(128)} %get-tuple-element.16.orders_ref, s32[48,3]{1,0:T(8,128)} %fusion.8.near_ref, f32[4,256]{1,0:T(4,128)} %pad_maximum_fusion.1.trig_ref, ...), custom_call_target="tpu_custom_call" | custom-call | tf_op jit(solution)/shard_map/operator_block/pallas_call | solution.py:793
  106.4 3.4 %settle.1 = (bf16[32,64,128]{2,1,0:T(8,128)(2,1)}, bf16[32,64,128]{2,1,0:T(8,128)(2,1)}) custom-call(bf16[32,64,128]{2,1,0:T(8,128)(2,1)} %get-tuple-element.6.first_in, bf16[32,64,128]{2,1,0:T(8,128)(2,1)} %get-tuple-element.7.second_in), custom_call_target="tpu_custom_call" | custom-call | tf_op jit(solution)/shard_map/settle/pallas_call | solution.py:834
  (5 shorter events, 0.1 us)
